TPU v7x, 32 devices: a whole 2x2x4 slice. The times are simulated.
32 devices in a mesh: seq: 16 (over z, y, x), dp: 2 (over core).
Axes of the slice: x: 2, y: 2, z: 4, core: 2. Of those that a mesh axis runs over, the one named last changes fastest.
Arguments:
- query_rows: bfloat16 [2, 2048, 4096], P('dp', 'seq'), may hold values from -6 to 6
- key_rows: bfloat16 [2, 2048, 4096], P('dp', 'seq'), may hold values from -6 to 6
- value_rows: bfloat16 [2, 2048, 4096], P('dp', 'seq'), may hold values from -6 to 6
- cotangent: bfloat16 [2, 2048, 4096], P('dp', 'seq'), may hold values from -6 to 6
- short_filter: float32 [3, 3, 4096], replicated, may hold values from -3 to 3
- residue: float32 [4096, 16], P('seq'), may hold values from -1.5 to 1.5
- decay_rate: float32 [4096, 16], P('seq'), as said below
Outputs:
- query_grad: bfloat16 [2, 2048, 4096], P('dp', 'seq')
- key_grad: bfloat16 [2, 2048, 4096], P('dp', 'seq')
- value_grad: bfloat16 [2, 2048, 4096], P('dp', 'seq')
- short_grad: float32 [3, 3, 4096], replicated
- residue_grad: float32 [4096, 16], P('seq')
- decay_grad: float32 [4096, 16], P('seq')
Inputs may be any that keep to these rules, and one draw needn't show every extreme that they name: `decay_rate`: every rate lies between 1 / 20480 and 1 / 32.
All inputs are finite; a program needn't handle non-finite values.
Results may differ from a plain program's by a relative error of at most 0.012.
Values may be sent and summed in bfloat16 or wider, within the bound.
A program may use at most 128 MiB of HBM per device.

v0:
```python
import math

import jax
import jax.numpy as jnp
from jax import lax
from jax.sharding import PartitionSpec as P

precise = lax.Precision.HIGH


def passed_along(shard, axis, by):
    count = lax.axis_size(axis)
    pairs = [(i, i + by) for i in range(count) if 0 <= i + by < count]
    return lax.ppermute(shard, axis, pairs)


def modal_impulse(residue, decay_rate, length):
    times = jnp.arange(length).astype(residue.dtype)
    weights = residue * jnp.sqrt(-jnp.expm1(-2.0 * decay_rate))
    return jnp.sum(weights[None] * jnp.exp(-decay_rate[None] * times[:, None, None]), axis=2)


def modal_pullback(residue, decay_rate, grad_impulse):
    length = grad_impulse.shape[0]
    times = jnp.arange(length).astype(residue.dtype)
    weighted = grad_impulse[:, :, None] * jnp.exp(-decay_rate[None] * times[:, None, None])
    first_sum = jnp.sum(weighted, axis=0)
    second_sum = jnp.sum(weighted * times[:, None, None], axis=0)
    root = jnp.sqrt(-jnp.expm1(-2.0 * decay_rate))
    residue_local = root * first_sum
    rate_local = (
        residue * jnp.exp(-2.0 * decay_rate) / root * first_sum - residue * root * second_sum
    )
    return (residue_local, rate_local)


def dft_tables(points):
    inner = points // 128
    freq_k = jnp.arange(65, dtype=jnp.int32)
    first = jnp.arange(64, dtype=jnp.int32)
    rows_b = jnp.arange(inner, dtype=jnp.int32)
    angle_one = 2.0 * math.pi / 128 * (first[:, None] * freq_k[None, :] % 128).astype(jnp.float32)
    fore_one = jnp.stack([jnp.cos(angle_one), -jnp.sin(angle_one)], axis=1)
    whole = freq_k[:, None, None] + 128 * rows_b[None, None, :]
    angle_two = (
        2.0 * math.pi / points * (rows_b[None, :, None] * whole % points).astype(jnp.float32)
    )
    cos_two = jnp.cos(angle_two)
    sin_two = jnp.sin(angle_two)
    fore_two = jnp.stack([jnp.stack([cos_two, -sin_two]), jnp.stack([sin_two, cos_two])])
    cos_back = cos_two.transpose(0, 2, 1)
    sin_back = sin_two.transpose(0, 2, 1)
    back_two = jnp.stack([jnp.stack([cos_back, sin_back]), jnp.stack([-sin_back, cos_back])])
    scaling = jnp.where((freq_k == 0) | (freq_k == 64), 1.0, 2.0).astype(jnp.float32) / points
    back_one = jnp.stack(
        [scaling[:, None] * jnp.cos(angle_one.T), -scaling[:, None] * jnp.sin(angle_one.T)]
    )
    return (fore_one, fore_two, back_two, back_one)


def forward_dft(signal, tables):
    fore_one, fore_two, back_two, back_one = tables
    inner = fore_two.shape[3]
    shaped = signal.reshape(signal.shape[0], 64, inner, signal.shape[-1])
    section_one = jnp.einsum("zabc,apk->zpkbc", shaped, fore_one, precision=precise)
    return jnp.einsum("zpkbc,pqkbm->zqkmc", section_one, fore_two, precision=precise)


def inverse_dft(spectrum, tables):
    fore_one, fore_two, back_two, back_one = tables
    inner = fore_two.shape[3]
    turned = jnp.einsum("zqkmc,qpkmb->zpkbc", spectrum, back_two, precision=precise)
    signal = jnp.einsum("zpkbc,pka->zabc", turned, back_one, precision=precise)
    return signal.reshape(signal.shape[0], 64 * inner, signal.shape[-1])


def complex_product(left, right, conjugate):
    left_real, left_imag = (left[:, 0], left[:, 1])
    right_real, right_imag = (right[:, 0], right[:, 1])
    if conjugate:
        right_imag = -right_imag
    return jnp.stack(
        [
            left_real * right_real - left_imag * right_imag,
            left_real * right_imag + left_imag * right_real,
        ],
        axis=1,
    )


def body(query_rows, key_rows, value_rows, cotangent, short_filter, residue, decay_rate):
    tokens = query_rows.shape[1]
    margin = short_filter.shape[1] - 1
    length = tokens * lax.axis_size("seq")
    tables = dft_tables(2 * length)
    stacked = jnp.stack([query_rows, key_rows, value_rows])
    before = passed_along(stacked[:, :, tokens - margin :, :], "seq", 1)
    widened = jnp.concatenate([before, stacked], axis=2)
    shorted = jnp.zeros(stacked.shape, jnp.float32)
    for offset in range(margin + 1):
        shorted = shorted + short_filter[:, offset][:, None, None, :] * widened[
            :, :, margin - offset : margin - offset + tokens, :
        ].astype(jnp.float32)
    query_short, key_short, value_short = (shorted[0], shorted[1], shorted[2])
    upstream = cotangent.astype(jnp.float32)
    gated = (key_short * value_short).astype(jnp.bfloat16)
    grad_mixed = (upstream * query_short).astype(jnp.bfloat16)
    impulse = modal_impulse(residue, decay_rate, length)
    impulse_spec = forward_dft(impulse[None], tables)
    gated_cols = lax.all_to_all(gated, "seq", split_axis=2, concat_axis=1, tiled=True)
    spectra = forward_dft(gated_cols.astype(jnp.float32), tables)
    mixed_cols = inverse_dft(complex_product(spectra, impulse_spec, False), tables)
    spectra, mixed_cols = (spectra, mixed_cols.astype(jnp.bfloat16))
    mixed = lax.all_to_all(mixed_cols, "seq", split_axis=1, concat_axis=2, tiled=True)
    grad_cols = lax.all_to_all(grad_mixed, "seq", split_axis=2, concat_axis=1, tiled=True)
    grad_spec = forward_dft(grad_cols.astype(jnp.float32), tables)
    grad_gated_cols = inverse_dft(complex_product(grad_spec, impulse_spec, True), tables)
    cross = jnp.sum(complex_product(grad_spec, spectra, True), axis=0, keepdims=True)
    grad_impulse = inverse_dft(cross, tables)[0]
    grad_gated_cols, grad_impulse = (grad_gated_cols.astype(jnp.bfloat16), grad_impulse)
    grad_gated = lax.all_to_all(grad_gated_cols, "seq", split_axis=1, concat_axis=2, tiled=True)
    grad_gated_wide = grad_gated.astype(jnp.float32)
    grad_short = jnp.stack(
        [
            upstream * mixed.astype(jnp.float32),
            grad_gated_wide * value_short,
            grad_gated_wide * key_short,
        ]
    )
    after = passed_along(grad_short[:, :, :margin, :], "seq", -1)
    trailing = jnp.concatenate([grad_short, after], axis=2)
    grad_inputs = jnp.zeros_like(grad_short)
    filter_terms = []
    for offset in range(margin + 1):
        grad_inputs = (
            grad_inputs
            + short_filter[:, offset][:, None, None, :]
            * trailing[:, :, offset : offset + tokens, :]
        )
        filter_terms.append(
            jnp.sum(
                grad_short
                * widened[:, :, margin - offset : margin - offset + tokens, :].astype(jnp.float32),
                axis=(1, 2),
            )
        )
    filter_local = jnp.stack(filter_terms, axis=1)
    residue_local, rate_local = modal_pullback(residue, decay_rate, grad_impulse)
    rate_local = decay_rate * rate_local
    factor = 1.0 / math.sqrt(query_rows.shape[0] * lax.axis_size("dp") * length)
    filter_grad = lax.psum(filter_local, ("seq", "dp"))
    residue_grad, decay_grad = lax.psum((residue_local, rate_local), "dp")
    return (
        grad_inputs[0].astype(jnp.bfloat16),
        grad_inputs[1].astype(jnp.bfloat16),
        grad_inputs[2].astype(jnp.bfloat16),
        filter_grad * factor,
        residue_grad * factor,
        decay_grad * factor,
    )


def solution(mesh):
    placed = (
        P("dp", "seq", None),
        P("dp", "seq", None),
        P("dp", "seq", None),
        P("dp", "seq", None),
        P(),
        P("seq", None),
        P("seq", None),
    )
    return jax.shard_map(
        body,
        mesh=mesh,
        in_specs=placed,
        out_specs=(
            P("dp", "seq", None),
            P("dp", "seq", None),
            P("dp", "seq", None),
            P(),
            P("seq", None),
            P("seq", None),
        ),
        check_vma=False,
    )
```

profile of v0, /device:TPU:0, one launch (start us, length us, event | category | flops | bytes accessed | tf_op | source)
XLA Modules:
  0.0 550.6 jit_solution(17202588535668053739)
XLA Ops:
  15.3 3.2 copy.146
  18.5 4.8 collective-permute-start
  25.9 2.8 copy.147
  28.7 6.2 %maximum_maximum_fusion = bf16[3,1,130,4096]{2,3,1,0:T(8,128)(2,1)S(1)} fusion(bf16[1,1,128,4096]{2,3,1,0:T(8,128)(2,1)S(1)} %bitcast.194, bf16[1,1,128,4096]{2,3,1,0:T(8,128)(2,1)S(1)} %bitcast.190, bf16[1,1,128,4096]{2,3,1,0:T(8,128)(2,1)S(1)} %bitcast.186, bf16[3,1,2,4096]{2,3,1,0:T(8,128)(2,1)} %copy.147), kind=kLoop, calls=%fused_computation.22 | loop fusion | flops 12779520 | bytes 6389760 | tf_op jit(solution)/shard_map/concatenate | solution.py:98
  35.0 6.4 %fusion.3 = f32[3,1,128,4096]{2,3,1,0:T(8,128)S(1)} fusion(f32[3,4096]{1,0:T(4,128)S(1)} %get-tuple-element.77, f32[3,4096]{1,0:T(4,128)S(1)} %get-tuple-element.78, f32[3,4096]{1,0:T(4,128)S(1)} %bitcast.216, bf16[3,1,130,4096]{2,3,1,0:T(8,128)(2,1)S(1)} %maximum_maximum_fusion, bf16[1,1,128,4096]{2,3,1,0:T(8,128)(2,1)S(1)} %bitcast.195, ...), kind=kLoop, calls=%fused_computation.13 | loop fusion | flops 15728640 | bytes 15876096 | tf_op jit(solution)/shard_map/add | solution.py:101
  44.0 16.7 %copy.251 = bf16[1,128,4096]{1,0,2:T(2,128)(2,1)S(1)} copy(bf16[1,128,4096]{1,2,0:T(8,128)(2,1)S(1)} %fusion.44) | data formatting | bytes 2097152 | tf_op jit(solution)/shard_map/convert_element_type | solution.py:107
  61.2 23.4 %reduce = bf16[4096,128]{1,0:T(8,128)(2,1)} reduce(bf16[4096,1,128]{2,1,0:T(2,128)(2,1)S(1)} %bitcast.202, bf16[]{:T(256)} %broadcast.536), dimensions={1}, to_apply=%bitcast.175.reduce_sub_computation | reduce | bytes 2097154
  86.7 7.3 %all-to-all-start.2 = ((bf16[16,2,16384]{2,1,0:T(2,128)(2,1)}), bf16[16,2,16384]{2,1,0:T(2,128)(2,1)}, u32[]{:S(2)}, u32[]{:S(2)}) async-start(bf16[16,2,16384]{2,1,0:T(2,128)(2,1)} %reshape.805), calls=%async_computation.2 | async-start | bytes 2097152 | tf_op jit(solution)/shard_map/all_to_all | solution.py:115
  96.4 16.7 %copy.253 = bf16[1,128,4096]{1,0,2:T(2,128)(2,1)S(1)} copy(bf16[1,128,4096]{1,2,0:T(8,128)(2,1)S(1)} %fusion.54) | data formatting | bytes 2097152 | tf_op jit(solution)/shard_map/convert_element_type | solution.py:106
  113.1 23.4 %reduce.1 = bf16[4096,128]{1,0:T(8,128)(2,1)} reduce(bf16[4096,1,128]{2,1,0:T(2,128)(2,1)S(1)} %bitcast.204, bf16[]{:T(256)} %broadcast.536), dimensions={1}, to_apply=%bitcast.177.reduce_sub_computation | reduce | bytes 2097154
  138.6 7.1 %all-to-all-start = ((bf16[16,2,16384]{2,1,0:T(2,128)(2,1)}), bf16[16,2,16384]{2,1,0:T(2,128)(2,1)}, u32[]{:S(2)}, u32[]{:S(2)}) async-start(bf16[16,2,16384]{2,1,0:T(2,128)(2,1)} %reshape.807), calls=%async_computation | async-start | bytes 2097152 | tf_op jit(solution)/shard_map/all_to_all | solution.py:110
  145.8 4.0 fusion.76
  152.2 4.9 copy.151
  159.0 4.8 copy.156
  165.3 4.3 reshape.806
  173.0 4.3 reshape.808
  178.4 10.9 %copy.149 = bf16[1,16,128,256]{3,2,1,0:T(8,128)(2,1)} copy(bf16[1,16,128,256]{2,3,1,0:T(8,128)(2,1)} %bitcast.209) | data formatting | bytes 2097152 | tf_op jit(solution)/shard_map/all_to_all | solution.py:110
  189.3 2.9 convolution_bitcast_fusion.1
  193.8 4.1 fusion.31
  198.0 4.1 fusion.37
  204.7 3.0 fusion.40
  207.7 3.7 fusion.51
  212.6 25.3 %multiply_reduce_fusion = (f32[256,16]{0,1:T(8,128)S(1)}, f32[256,16]{0,1:T(8,128)S(1)}, f32[2048,256]{1,0:T(8,128)S(1)}) fusion(f32[2048,256]{1,0:T(8,128)S(1)} %bitcast.215, f32[2048]{0:T(1024)S(1)} %copy-done.20, f32[256,16]{0,1:T(8,128)S(1)} %copy-done.19, f32[256,16]{0,1:T(8,128)S(1)} %get-tuple-element.67), kind=kLoop, calls=%fused_computation | loop fusion | flops 58187776 | bytes 4268032 | tf_op jit(solution)/shard_map/reduce_sum | solution.py:28
  237.9 3.0 convolution_bitcast_fusion.2
  240.9 5.8 %fusion.34 = f32[1,2,65,32,256]{4,3,1,2,0:T(8,128)} fusion(f32[2,2,65,32,32]{3,4,0,1,2:T(8,128)S(1)} %bitcast.182, f32[2,65,32,256,1]{3,1,2,0,4:T(8,128)S(1)} %convolution_bitcast_fusion.2), kind=kOutput, calls=%fused_computation.55 | convolution fusion | flops 408944640 | bytes 9584640 | tf_op jit(solution)/shard_map/zpkbc,pqkbm->zqkmc/dot_general | solution.py:66
  246.7 8.8 %multiply_subtract_fusion.2 = (f32[1,1,65,32,256]{4,3,1,2,0:T(8,128)}, f32[1,1,65,32,256]{4,3,1,2,0:T(8,128)}, f32[1,1,65,32,256]{4,3,1,2,0:T(8,128)S(1)}, f32[1,1,65,32,256]{4,3,1,2,0:T(8,128)S(1)}) fusion(f32[1,2,65,32,256]{4,3,1,2,0:T(8,128)} %fusion.34, f32[1,2,65,32,256]{4,3,1,2,0:T(8,128)} %copy-done.2, f32[1,2,65,32,256]{4,3,1,2,0:T(8,128)} %copy-done.3), kind=kLoop, calls=%fused_computation.65 | loop fusion | flops 6922240 | bytes 21299200 | tf_op jit(solution)/shard_map/sub | solution.py:84
  258.0 3.9 bitcast_convert_fusion
  262.4 11.7 %copy.250 = bf16[1,2048,256]{2,0,1:T(2,128)(2,1)S(1)} copy(bf16[1,2048,256]{2,1,0:T(8,128)(2,1)S(1)} %bitcast.210) | data formatting | bytes 2097152 | tf_op jit(solution)/shard_map/convert_element_type | solution.py:120
  274.2 11.6 %reduce.2 = bf16[2048,256]{1,0:T(8,128)(2,1)} reduce(bf16[2048,1,256]{2,1,0:T(2,128)(2,1)S(1)} %bitcast.205, bf16[]{:T(256)} %broadcast.536), dimensions={1}, to_apply=%bitcast.174.reduce_sub_computation | reduce | bytes 2097154
  287.9 6.9 %all-to-all-start.3 = ((bf16[16,2,16384]{2,1,0:T(2,128)(2,1)}), bf16[16,2,16384]{2,1,0:T(2,128)(2,1)}, u32[]{:S(2)}, u32[]{:S(2)}) async-start(bf16[16,2,16384]{2,1,0:T(2,128)(2,1)} %reshape.809), calls=%async_computation.3 | async-start | bytes 2097152 | tf_op jit(solution)/shard_map/all_to_all | solution.py:121
  294.8 6.1 %fusion.42 = f32[2,65,32,256]{3,2,1,0:T(8,128)S(1)} fusion(f32[2,2,65,32,32]{3,4,0,2,1:T(8,128)} %copy.156, f32[1,1,65,32,256]{4,3,1,2,0:T(8,128)} %get-tuple-element.45, f32[1,1,65,32,256]{4,3,1,2,0:T(8,128)} %get-tuple-element.44), kind=kOutput, calls=%fused_computation.59 | convolution fusion | flops 410009600 | bytes 9584640 | tf_op jit(solution)/shard_map/zqkmc,qpkmb->zpkbc/dot_general | solution.py:72
  300.9 3.7 bitcast_convert_fusion.1
  305.2 11.7 %copy.252 = bf16[1,2048,256]{2,0,1:T(2,128)(2,1)S(1)} copy(bf16[1,2048,256]{2,1,0:T(8,128)(2,1)S(1)} %bitcast.211) | data formatting | bytes 2097152 | tf_op jit(solution)/shard_map/convert_element_type | solution.py:113
  317.0 11.6 %reduce.3 = bf16[2048,256]{1,0:T(8,128)(2,1)} reduce(bf16[2048,1,256]{2,1,0:T(2,128)(2,1)S(1)} %bitcast.203, bf16[]{:T(256)} %broadcast.536), dimensions={1}, to_apply=%bitcast.176.reduce_sub_computation | reduce | bytes 2097154
  330.7 6.9 %all-to-all-start.1 = ((bf16[16,2,16384]{2,1,0:T(2,128)(2,1)}), bf16[16,2,16384]{2,1,0:T(2,128)(2,1)}, u32[]{:S(2)}, u32[]{:S(2)}) async-start(bf16[16,2,16384]{2,1,0:T(2,128)(2,1)} %reshape.811), calls=%async_computation.1 | async-start | bytes 2097152 | tf_op jit(solution)/shard_map/all_to_all | solution.py:114
  337.7 3.4 all-reduce
  341.7 4.5 reshape.810
  348.4 4.5 bitcast_multiply_fusion.1
  353.0 7.3 %all-to-all-done.1 = bf16[16,2,16384]{2,1,0:T(2,128)(2,1)} async-done(((bf16[16,2,16384]{2,1,0:T(2,128)(2,1)}), bf16[16,2,16384]{2,1,0:T(2,128)(2,1)}, u32[]{:S(2)}, u32[]{:S(2)}) %all-to-all-start.1) | async-done | bytes 1048608 | tf_op jit(solution)/shard_map/all_to_all | solution.py:114
  360.2 5.8 %reshape.812 = bf16[2048,1,256]{2,1,0:T(2,128)(2,1)} reshape(bf16[16,2,16384]{2,1,0:T(2,128)(2,1)} %all-to-all-done.1) | data formatting | bytes 2097152
  369.4 3.0 copy.161
  374.9 3.0 pad_maximum_fusion.1
  378.0 4.4 copy.173
  384.3 4.6 collective-permute-done.1
  388.9 4.0 copy.174
  392.9 6.1 %pad_maximum_fusion = f32[3,1,130,4096]{2,3,1,0:T(8,128)S(1)} fusion(f32[3,1,2,4096]{2,3,1,0:T(8,128)} %copy.174, f32[1,1,128,4096]{2,3,1,0:T(8,128)} %get-tuple-element.51, f32[1,1,128,4096]{2,3,1,0:T(8,128)} %copy-done.4, f32[1,1,128,4096]{2,3,1,0:T(8,128)} %copy-done.8), kind=kLoop, calls=%fused_computation.5 | loop fusion | flops 4792320 | bytes 12779520 | tf_op jit(solution)/shard_map/concatenate | solution.py:131
  401.2 16.4 %fusion.5 = (f32[3,4096]{1,0:T(4,128)S(1)}, f32[3,4096]{1,0:T(4,128)S(1)}, f32[3,4096]{1,0:T(4,128)S(1)}, bf16[3,1,128,4096]{2,3,1,0:T(8,128)(2,1)}) fusion(bf16[3,1,130,4096]{2,3,1,0:T(8,128)(2,1)S(1)} %bitcast.184, f32[1,1,128,4096]{2,3,1,0:T(8,128)S(1)} %copy-done.7, f32[1,1,128,4096]{2,3,1,0:T(8,128)S(1)} %copy-done.5, ...), kind=kLoop, calls=%fused_computation.15 | loop fusion | flops 29847552 | bytes 31752192 | tf_op jit(solution)/shard_map/reduce_sum | solution.py:141
  424.3 117.5 %all-reduce.3.cloned.1.call-done = f32[3,3,4096]{2,0,1:T(4,128)} async-done(((f32[3,3,4096]{2,0,1:T(4,128)}), f32[3,3,4096]{2,0,1:T(4,128)}) %all-reduce.3.cloned.1.call-update) | async-done | bytes 147472 | tf_op jit(solution)/shard_map/psum | solution.py:151
  (116 shorter events, 65.2 us)
Async XLA Ops:
  10.4 24.6 %copy-start.10 = (bf16[1,128,4096]{1,2,0:T(8,128)(2,1)}, bf16[1,128,4096]{1,2,0:T(8,128)(2,1)S(1)}, u32[]{:S(2)}) copy-start(bf16[1,128,4096]{1,2,0:T(8,128)(2,1)S(1)} %copy.144) | copy-start | bytes 3145732
  12.4 22.6 %copy-start.12 = (bf16[1,128,4096]{1,2,0:T(8,128)(2,1)}, bf16[1,128,4096]{1,2,0:T(8,128)(2,1)S(1)}, u32[]{:S(2)}) copy-start(bf16[1,128,4096]{1,2,0:T(8,128)(2,1)S(1)} %copy.145) | copy-start | bytes 3145732
  12.8 10.6 %copy-start.16 = (f32[3,3,4096]{2,1,0:T(4,128)S(1)}, f32[3,3,4096]{2,1,0:T(4,128)}, u32[]{:S(2)}) copy-start(f32[3,3,4096]{2,1,0:T(4,128)} %param.11) | copy-start | bytes 442372
  18.5 7.4 %collective-permute-start = (bf16[3,1,2,4096]{3,2,1,0:T(2,128)(2,1)S(1)}, bf16[3,1,2,4096]{3,2,1,0:T(2,128)(2,1)S(1)}, u32[]{:S(2)}, u32[]{:S(2)}) collective-permute-start(bf16[3,1,2,4096]{3,2,1,0:T(2,128)(2,1)S(1)} %copy.146), channel_id=1, source_target_pairs={{0,2},{2,4},{4,6},{6,8},{8,10},{10,12},{12,14},{14,16},{16,18},{18... | collective-permute-start | bytes 147464 | tf_op jit(solution)/shard_map/ppermute | solution.py:14
  35.0 6.4 %copy-start = (bf16[3,1,130,4096]{2,3,1,0:T(8,128)(2,1)}, bf16[3,1,130,4096]{2,3,1,0:T(8,128)(2,1)S(1)}, u32[]{:S(2)}) copy-start(bf16[3,1,130,4096]{2,3,1,0:T(8,128)(2,1)S(1)} %maximum_maximum_fusion) | copy-start | bytes 9584644
  35.0 6.4 %copy-start.14 = (bf16[1,128,4096]{1,2,0:T(8,128)(2,1)S(1)}, bf16[1,128,4096]{1,2,0:T(8,128)(2,1)}, u32[]{:S(2)}) copy-start(bf16[1,128,4096]{1,2,0:T(8,128)(2,1)} %copy.142) | copy-start | bytes 3145732
  41.4 2.6 copy-start.1
  86.7 51.9 %all-to-all-start.2 = ((bf16[16,2,16384]{2,1,0:T(2,128)(2,1)}), bf16[16,2,16384]{2,1,0:T(2,128)(2,1)}, u32[]{:S(2)}, u32[]{:S(2)}) async-start(bf16[16,2,16384]{2,1,0:T(2,128)(2,1)} %reshape.805), calls=%async_computation.2 | async-start | bytes 2097152 | tf_op jit(solution)/shard_map/all_to_all | solution.py:115
  138.6 34.3 %all-to-all-start = ((bf16[16,2,16384]{2,1,0:T(2,128)(2,1)}), bf16[16,2,16384]{2,1,0:T(2,128)(2,1)}, u32[]{:S(2)}, u32[]{:S(2)}) async-start(bf16[16,2,16384]{2,1,0:T(2,128)(2,1)} %reshape.807), calls=%async_computation | async-start | bytes 2097152 | tf_op jit(solution)/shard_map/all_to_all | solution.py:110
  158.9 5.5 %copy-start.17 = (f32[256,16]{0,1:T(8,128)S(1)}, f32[256,16]{0,1:T(8,128)}, u32[]{:S(2)}) copy-start(f32[256,16]{0,1:T(8,128)} %param.12) | copy-start | bytes 49156
  158.9 5.5 %copy-start.18 = (f32[256,16]{0,1:T(8,128)S(1)}, f32[256,16]{0,1:T(8,128)}, u32[]{:S(2)}) copy-start(f32[256,16]{0,1:T(8,128)} %param.13) | copy-start | bytes 49156
  178.4 13.8 %copy-start.15 = (bf16[1,16,128,256]{3,2,1,0:T(8,128)(2,1)S(1)}, bf16[1,16,128,256]{3,2,1,0:T(8,128)(2,1)}, u32[]{:S(2)}) copy-start(bf16[1,16,128,256]{3,2,1,0:T(8,128)(2,1)} %copy.163) | copy-start | bytes 3145732
  178.4 15.4 %slice-start.2 = ((s8[4259840]{0:T(1024)(128)(4,1)}), s8[65536]{0:T(1024)(128)(4,1)S(1)}, s32[]{:S(2)}) async-start(s8[4259840]{0:T(1024)(128)(4,1)} %bitcast.181), calls=%async_computation.7 | async-start | bytes 131072
  189.2 4.6 slice-start.3
  197.9 4.1 copy-start.2
  197.9 6.7 %slice-start = ((s8[4259840]{0:T(1024)(128)(4,1)}), s8[4194304]{0:T(1024)(128)(4,1)S(1)}, s32[]{:S(2)}) async-start(s8[4259840]{0:T(1024)(128)(4,1)} %bitcast.179), calls=%async_computation.5 | async-start | bytes 8388608
  202.1 2.6 copy-start.3
  202.1 2.6 slice-start.1
  207.6 4.9 copy-start.19
  207.7 4.9 copy-start.20
  287.9 42.8 %all-to-all-start.3 = ((bf16[16,2,16384]{2,1,0:T(2,128)(2,1)}), bf16[16,2,16384]{2,1,0:T(2,128)(2,1)}, u32[]{:S(2)}, u32[]{:S(2)}) async-start(bf16[16,2,16384]{2,1,0:T(2,128)(2,1)} %reshape.809), calls=%async_computation.3 | async-start | bytes 2097152 | tf_op jit(solution)/shard_map/all_to_all | solution.py:121
  330.7 29.6 %all-to-all-start.1 = ((bf16[16,2,16384]{2,1,0:T(2,128)(2,1)}), bf16[16,2,16384]{2,1,0:T(2,128)(2,1)}, u32[]{:S(2)}, u32[]{:S(2)}) async-start(bf16[16,2,16384]{2,1,0:T(2,128)(2,1)} %reshape.811), calls=%async_computation.1 | async-start | bytes 2097152 | tf_op jit(solution)/shard_map/all_to_all | solution.py:114
  337.6 204.2 %all-reduce.3.cloned.1.call-start = ((), (), s32[]{:S(2)}) async-start(), calls=%async_computation.4 | async-start | bytes 393216 | tf_op jit(solution)/shard_map/psum | solution.py:151
  353.0 21.7 %copy-start.4 = (f32[1,1,128,4096]{2,3,1,0:T(8,128)}, f32[1,1,128,4096]{2,3,1,0:T(8,128)S(1)}, u32[]{:S(2)}) copy-start(f32[1,1,128,4096]{2,3,1,0:T(8,128)S(1)} %get-tuple-element.50) | copy-start | bytes 6291460
  372.4 2.5 copy-start.6
  374.6 3.3 copy-start.8
  382.4 6.5 %collective-permute-start.1 = (f32[3,1,2,4096]{3,2,1,0:T(2,128)S(1)}, f32[3,1,2,4096]{3,2,1,0:T(2,128)S(1)}, u32[]{:S(2)}, u32[]{:S(2)}) collective-permute-start(f32[3,1,2,4096]{3,2,1,0:T(2,128)S(1)} %copy.173), channel_id=1, source_target_pairs={{2,0},{4,2},{6,4},{8,6},{10,8},{12,10},{14,12},{16,14},{18,16},{20... | collective-permute-start | bytes 294920 | tf_op jit(solution)/shard_map/ppermute | solution.py:14
  388.9 10.2 %slice-start.4 = ((s8[6291456]{0:T(1024)(128)(4,1)}), s8[2097152]{0:T(1024)(128)(4,1)S(1)}, s32[]{:S(2)}) async-start(s8[6291456]{0:T(1024)(128)(4,1)} %bitcast.183), calls=%async_computation.9 | async-start | bytes 4194304
  392.9 6.2 %slice-start.5 = ((s8[6291456]{0:T(1024)(128)(4,1)}), s8[4194304]{0:T(1024)(128)(4,1)S(1)}, s32[]{:S(2)}) async-start(s8[6291456]{0:T(1024)(128)(4,1)} %bitcast.183), calls=%async_computation.10 | async-start | bytes 8388608
  392.9 6.5 %copy-start.5 = (f32[1,1,128,4096]{2,3,1,0:T(8,128)S(1)}, f32[1,1,128,4096]{2,3,1,0:T(8,128)}, u32[]{:S(2)}) copy-start(f32[1,1,128,4096]{2,3,1,0:T(8,128)} %copy-done.4) | copy-start | bytes 6291460
  392.9 7.1 %copy-start.7 = (f32[1,1,128,4096]{2,3,1,0:T(8,128)S(1)}, f32[1,1,128,4096]{2,3,1,0:T(8,128)}, u32[]{:S(2)}) copy-start(f32[1,1,128,4096]{2,3,1,0:T(8,128)} %get-tuple-element.51) | copy-start | bytes 6291460
  392.9 7.7 %copy-start.9 = (f32[1,1,128,4096]{2,3,1,0:T(8,128)S(1)}, f32[1,1,128,4096]{2,3,1,0:T(8,128)}, u32[]{:S(2)}) copy-start(f32[1,1,128,4096]{2,3,1,0:T(8,128)} %copy-done.8) | copy-start | bytes 6291460
  392.9 7.9 %copy-start.11 = (bf16[1,128,4096]{1,2,0:T(8,128)(2,1)S(1)}, bf16[1,128,4096]{1,2,0:T(8,128)(2,1)}, u32[]{:S(2)}) copy-start(bf16[1,128,4096]{1,2,0:T(8,128)(2,1)} %copy-done.10) | copy-start | bytes 3145732
  392.9 8.2 %copy-start.13 = (bf16[1,128,4096]{1,2,0:T(8,128)(2,1)S(1)}, bf16[1,128,4096]{1,2,0:T(8,128)(2,1)}, u32[]{:S(2)}) copy-start(bf16[1,128,4096]{1,2,0:T(8,128)(2,1)} %copy-done.12) | copy-start | bytes 3145732
Sparse Core Ops, SparseCore 0:
  418.5 123.2 all-reduce.2
where the time goes:
time: 556 us; the launch traced here: 551 us
  other arithmetic  168 us (30%)
  local copies, waits for them, and re-layouts  157 us (28%)
  waiting for transfers between devices  129 us (23%)
  matrix products  44.2 us (8%)
  starting transfers between devices  34.3 us (6%)
  between operations  15 us (3%)
    psum x1, waiting for transfers between devices, body(): filter_grad = lax.psum(filter_local, ('seq', 'dp'))  117 us
    unnamed x7, other arithmetic  69.9 us
    unnamed x75, local copies, waits for them, and re-layouts  48.6 us
    reduce_sum x1, other arithmetic, modal_pullback(): second_sum = jnp.sum(weighted * times[:, None, None], axis=0)  25.3 us
    convert_element_type x1, local copies, waits for them, and re-layouts, body(): gated = (key_short * value_short).astype(jnp.bfloat16)  16.7 us
    convert_element_type x1, local copies, waits for them, and re-layouts, body(): grad_mixed = (upstream * query_short).astype(jnp.bfloat16)  16.7 us
    reduce_sum x1, other arithmetic, body(): jnp.sum(grad_short * widened[:, :, margin - offset:margin - offset + toke...  16.4 us
    dot_general x3, matrix products, forward_dft(): jnp.einsum('zpkbc,pqkbm->zqkmc', section_one, fore_two, precision=precise)  14 us
  transfers between devices with their start and end apart: 7, of which 3 were waited for; matrix products, arithmetic and copies ran while one was open for 23% of the time, Pallas kernels for 0%

commit v1 on v0

v1 whole, which is shorter than its diff:
```python
import functools
import math

import jax
import jax.numpy as jnp
from jax import lax
from jax.experimental import pallas as pl
from jax.experimental.pallas import tpu as pltpu
from jax.sharding import PartitionSpec as P

LANES = 128
GROUPS = 8
WIDE = LANES * GROUPS
F32 = jnp.float32
BF16 = jnp.bfloat16


def row(t):
    start = t * GROUPS
    if not isinstance(t, int):
        start = pl.multiple_of(start, GROUPS)
    return pl.ds(start, GROUPS)


def rounded(values):
    return values.astype(BF16).astype(F32)


def spread_rows(source, target, shift, tokens):
    def step(i, carry):
        start = pl.multiple_of(i * 16, 16)
        for s in range(GROUPS):
            piece = source[0, pl.ds(start, 16), s * LANES : (s + 1) * LANES].astype(F32)
            target[pl.ds((start + shift) * GROUPS + s, 16, stride=GROUPS), :] = piece
        return carry

    lax.fori_loop(0, tokens // 16, step, 0)


def gather_rows(source, target, tokens):
    def step(i, carry):
        start = pl.multiple_of(i * 16, 16)
        for s in range(GROUPS):
            piece = source[pl.ds(start * GROUPS + s, 16, stride=GROUPS), :]
            target[0, pl.ds(start, 16), s * LANES : (s + 1) * LANES] = piece.astype(BF16)
        return carry

    lax.fori_loop(0, tokens // 16, step, 0)


def load_inputs(tokens, margin, rows, before, after, wide):
    for i in range(4):
        spread_rows(rows[i], wide[i], margin, tokens)
        for j in range(margin):
            if i < 3:
                wide[i][row(j), :] = before[i, j].astype(F32)
            wide[i][row(margin + tokens + j), :] = after[i, j].astype(F32)


def short_products(tokens, margin, taps, wide, gated, grad_mixed, keep):
    weights = [[taps[i, j] for j in range(margin + 1)] for i in range(3)]

    def step(t, carry):
        shorted = []
        for i in range(3):
            total = weights[i][0] * wide[i][row(t + margin), :]
            for j in range(1, margin + 1):
                total = total + weights[i][j] * wide[i][row(t + margin - j), :]
            shorted.append(total)
        gated[row(t), :] = rounded(shorted[1] * shorted[2])
        grad_mixed[row(t), :] = rounded(wide[3][row(t + margin), :] * shorted[0])
        if keep is not None:
            keep[0][row(t), :] = shorted[1]
            keep[1][row(t), :] = shorted[2]
        return carry

    lax.fori_loop(0, tokens + margin, step, 0, unroll=2)


def ends_kernel(tokens, margin, modes, q, k, v, c, before, after, taps, rate, state, w0, w1, w2, w3, gated, grad_mixed):
    wide = (w0, w1, w2, w3)
    load_inputs(tokens, margin, (q, k, v, c), before, after, wide)
    short_products(tokens, margin, taps, wide, gated, grad_mixed, None)
    decay = [jnp.exp(-rate[n]) for n in range(modes)]
    zero = jnp.zeros((GROUPS, LANES), F32)

    def step(t, carry):
        ahead, back = carry
        u = gated[row(t), :]
        g = grad_mixed[row(tokens - 1 - t), :]
        return (
            tuple(decay[n] * ahead[n] + u for n in range(modes)),
            tuple(decay[n] * back[n] + g for n in range(modes)),
        )

    ahead, back = lax.fori_loop(0, tokens, step, ((zero,) * modes, (zero,) * modes), unroll=2)
    for n in range(modes):
        state[n, 0, 0] = ahead[n]
        state[n, 0, 1] = back[n]


def main_kernel(
    tokens, margin, modes, part, q, k, v, c, before, after, taps, rate, weight, state,
    dq, dk, dv, sums, tap_sums,
    w0, w1, w2, w3, gated, grad_mixed, keys, values, mixed, grad_gated, trail, o0, o1, o2,
):
    wide = (w0, w1, w2, w3)
    load_inputs(tokens, margin, (q, k, v, c), before, after, wide)
    short_products(tokens, margin, taps, wide, gated, grad_mixed, (keys, values))
    zero = jnp.zeros((GROUPS, LANES), F32)
    for first in range(0, modes, part):
        some = range(first, first + part)
        decay = [jnp.exp(-rate[n]) for n in some]
        amount = [weight[n] for n in some]

        def total_of(terms):
            terms = list(terms)
            while len(terms) > 1:
                terms = [a + b for a, b in zip(terms[::2], terms[1::2])]
            return terms[0]

        def forward(t, carry):
            x, dots = carry
            u = gated[row(t), :]
            g = grad_mixed[row(t), :]
            x = tuple(decay[n] * x[n] + u for n in range(part))
            for n in range(part):
                trail[row(t * part + n), :] = x[n]
            y = total_of(amount[n] * x[n] for n in range(part))
            if first > 0:
                y = y + mixed[row(t), :]
            mixed[row(t), :] = y
            return (x, tuple(dots[n] + g * x[n] for n in range(part)))

        start = tuple(state[n, 0, 0] for n in some)
        x, dots = lax.fori_loop(0, tokens, forward, (start, (zero,) * part), unroll=2)
        for n in range(part):
            sums[0, first + n] = dots[n]
        for t in range(tokens, tokens + margin):
            u = gated[row(t), :]
            x = tuple(decay[n] * x[n] + u for n in range(part))
            y = total_of(amount[n] * x[n] for n in range(part))
            if first > 0:
                y = y + mixed[row(t), :]
            mixed[row(t), :] = y

        def backward(i, carry):
            t = tokens - 1 - i
            h, dots = carry
            g = grad_mixed[row(t), :]
            dots = tuple(dots[n] + trail[row(t * part + n), :] * h[n] for n in range(part))
            h = tuple(decay[n] * h[n] + g for n in range(part))
            y = total_of(amount[n] * h[n] for n in range(part))
            if first > 0:
                y = y + grad_gated[row(t), :]
            grad_gated[row(t), :] = y
            return (h, dots)

        start = tuple(state[n, 0, 1] for n in some)
        h, dots = lax.fori_loop(0, tokens, backward, (start, (zero,) * part), unroll=2)
        for n in range(part):
            sums[1, first + n] = decay[n] * dots[n]
        grow = [jnp.exp(rate[n]) for n in some]
        h = start
        for t in range(tokens, tokens + margin):
            y = total_of(amount[n] * h[n] for n in range(part))
            if first > 0:
                y = y + grad_gated[row(t), :]
            grad_gated[row(t), :] = y
            g = grad_mixed[row(t), :]
            h = tuple((h[n] - g) * grow[n] for n in range(part))

    filters = [[taps[i, j] for j in range(margin + 1)] for i in range(3)]
    outs = (o0, o1, o2)

    def grads_at(t):
        m = rounded(mixed[row(t), :])
        gg = rounded(grad_gated[row(t), :])
        return (wide[3][row(t + margin), :] * m, gg * values[row(t), :], gg * keys[row(t), :])

    def finish(i, carry):
        t = tokens - 1 - i
        later, dots = carry
        now = grads_at(t)
        window = (now,) + later
        new = []
        for a in range(3):
            total = filters[a][0] * now[a]
            for j in range(1, margin + 1):
                total = total + filters[a][j] * window[j][a]
            outs[a][row(t), :] = total
            for j in range(margin + 1):
                new.append(dots[a * (margin + 1) + j] + now[a] * wide[a][row(t + margin - j), :])
        return (window[:margin], tuple(new))

    later = tuple(grads_at(tokens + j) for j in range(margin))
    later, dots = lax.fori_loop(0, tokens, finish, (later, (zero,) * (3 * (margin + 1))), unroll=2)
    for a in range(3):
        for j in range(margin + 1):
            tap_sums[a, j] = dots[a * (margin + 1) + j]
    for source, target in zip(outs, (dq, dk, dv)):
        gather_rows(source, target, tokens)


def carry_kernel(count, power, got, out):
    factor = power[...]
    ahead = jnp.zeros_like(factor)
    back = jnp.zeros_like(factor)
    for p in range(count):
        out[p, 0] = ahead
        ahead = factor * ahead + got[p, 0]
        out[count - 1 - p, 1] = back
        back = factor * back + got[count - 1 - p, 1]


def swap(blocks):
    return lax.all_to_all(blocks, "seq", split_axis=0, concat_axis=0, tiled=True)


def passed_along(shard, axis, by):
    count = lax.axis_size(axis)
    pairs = [(i, i + by) for i in range(count) if 0 <= i + by < count]
    return lax.ppermute(shard, axis, pairs)


def body(query_rows, key_rows, value_rows, cotangent, short_filter, residue, decay_rate):
    batch, tokens, width = query_rows.shape
    assert batch == 1
    margin = short_filter.shape[1] - 1
    modes = residue.shape[1]
    count = lax.axis_size("seq")
    own = residue.shape[0] // LANES
    tiles = width // LANES
    split = count // modes
    assert split * modes == count
    per = tiles // split // GROUPS
    blocks = width // WIDE
    length = tokens * count
    vmem = 56 << 20

    root = jnp.sqrt(-jnp.expm1(-2.0 * decay_rate))
    mine = jnp.stack([decay_rate.T, (residue * root).T]).reshape(2, modes, own, LANES)
    everyone = lax.all_gather(mine, "seq")
    rate, weight = everyone.transpose(1, 2, 0, 3, 4).reshape(2, modes, tiles, LANES)

    rows = (query_rows, key_rows, value_rows, cotangent)
    before = jnp.stack([x[0, tokens - margin :] for x in rows[:3]])
    before = passed_along(before, "seq", 1).reshape(3, margin, tiles, LANES)
    after = jnp.stack([x[0, :margin] for x in rows])
    after = passed_along(after, "seq", -1).reshape(4, margin, tiles, LANES)
    taps = short_filter.reshape(3, margin + 1, tiles, LANES)

    rows_spec = pl.BlockSpec((1, tokens, WIDE), lambda i: (0, 0, i))

    def tile_spec(*lead):
        zeros = (0,) * len(lead)
        return pl.BlockSpec(lead + (GROUPS, LANES), lambda i: zeros + (i, 0))

    state_spec = pl.BlockSpec(
        (modes, 1, 2, GROUPS, LANES), lambda i: (0, i // per, 0, i % per, 0)
    )

    def scratch(n):
        return pltpu.VMEM((n * GROUPS, LANES), F32)

    params = pltpu.CompilerParams(vmem_limit_bytes=vmem)
    head = [rows_spec] * 4 + [tile_spec(3, margin), tile_spec(4, margin), tile_spec(3, margin + 1), tile_spec(modes)]
    wide = [scratch(tokens + 2 * margin)] * 4
    state = pl.pallas_call(
        functools.partial(ends_kernel, tokens, margin, modes),
        grid=(blocks,),
        in_specs=head,
        out_specs=state_spec,
        out_shape=jax.ShapeDtypeStruct((modes, split, 2, tiles // split, LANES), F32),
        scratch_shapes=wide + [scratch(tokens + margin)] * 2,
        compiler_params=params,
        name="block_ends",
    )(*rows, before, after, taps, rate)

    got = swap(state.reshape(count, 2, tiles // split, LANES))
    slices = rate.reshape(count, tiles // split, LANES)
    power = jnp.exp(-tokens * lax.dynamic_index_in_dim(slices, lax.axis_index("seq"), 0, False))
    carried = pl.pallas_call(
        functools.partial(carry_kernel, count),
        out_shape=jax.ShapeDtypeStruct(got.shape, F32),
        name="carries",
    )(power, got)
    state = swap(carried).reshape(state.shape)

    shapes = [jax.ShapeDtypeStruct(query_rows.shape, BF16)] * 3
    dq, dk, dv, sums, tap_sums = pl.pallas_call(
        functools.partial(main_kernel, tokens, margin, modes, modes // 2),
        grid=(blocks,),
        in_specs=head + [tile_spec(modes), state_spec],
        out_specs=[rows_spec] * 3 + [tile_spec(2, modes), tile_spec(3, margin + 1)],
        out_shape=shapes
        + [
            jax.ShapeDtypeStruct((2, modes, tiles, LANES), F32),
            jax.ShapeDtypeStruct((3, margin + 1, tiles, LANES), F32),
        ],
        scratch_shapes=wide
        + [scratch(tokens + margin)] * 6
        + [scratch(tokens * modes // 2)]
        + [scratch(tokens)] * 3,
        compiler_params=params,
        name="mixer",
    )(*rows, before, after, taps, rate, weight, state)

    terms = 2 * modes + 3 * (margin + 1)
    packed = jnp.concatenate(
        [sums.reshape(2 * modes, count, own, LANES), tap_sums.reshape(-1, count, own, LANES)]
    ).transpose(1, 0, 2, 3)
    reduced = lax.psum(jnp.sum(swap(packed), axis=0), "dp")
    factor = 1.0 / math.sqrt(batch * lax.axis_size("dp") * length)
    reduced = reduced * factor
    filter_grad = lax.all_gather(reduced[2 * modes :], "seq", axis=1)
    filter_grad = filter_grad.reshape(3, margin + 1, width)
    first_sum, second_sum = (
        reduced[: 2 * modes].reshape(2, modes, own * LANES).transpose(0, 2, 1)
    )
    residue_grad = root * first_sum
    rate_grad = (
        residue * jnp.exp(-2.0 * decay_rate) / root * first_sum - residue * root * second_sum
    )
    return (dq, dk, dv, filter_grad, residue_grad, decay_rate * rate_grad)


def solution(mesh):
    rows = P("dp", "seq", None)
    modes = P("seq", None)
    return jax.shard_map(
        body,
        mesh=mesh,
        in_specs=(rows, rows, rows, rows, P(), modes, modes),
        out_specs=(rows, rows, rows, P(), modes, modes),
        check_vma=False,
    )
```

time: 556 us -> 203 us (0.37)
  other arithmetic: 168 us -> 3.85 us
  local copies, waits for them, and re-layouts: 157 us -> 8.88 us
  waiting for transfers between devices: 129 us -> 9.4 us
  blocking collectives: 3.41 us -> 119 us
  Pallas kernels: 0 us -> 49.8 us
  matrix products: 44.2 us -> 0 us
  starting transfers between devices: 34.3 us -> 9.71 us
  between operations: 15 us -> 0.79 us
    psum x1 -> x0, waiting for transfers between devices: 117 us -> none  [body(): filter_grad = lax.psum(filter_local, ('seq', 'dp'))]
    all_gather x0 -> x2, blocking collectives: none -> 83.7 us  [the longest x1 45.2 us: body(): everyone = lax.all_gather(mine, 'seq')]
    unnamed x7 -> x0, other arithmetic: 69.9 us -> none
    convert_element_type x9 -> x0, local copies, waits for them, and re-layouts: 64.9 us -> none  [the longest x1 16.7 us: body(): gated = (key_short * value_short).astype(jnp.bfloat16)]
    pallas_call x0 -> x3, Pallas kernels: none -> 49.8 us  [the longest x1 34.4 us: body(): pl.pallas_call(functools.partial(main_kernel, tokens, margin, modes, mode...]
    unnamed x75 -> x10, local copies, waits for them, and re-layouts: 48.6 us -> 2.24 us
    dot_general x12 -> x0, matrix products: 44.2 us -> none  [the longest x3 14 us: forward_dft(): jnp.einsum('zpkbc,pqkbm->zqkmc', section_one, fore_two, precision=precise)]
    reduce_sum x2 -> x1, other arithmetic: 41.8 us -> 0.21 us  [body(): reduced = lax.psum(jnp.sum(swap(packed), axis=0), 'dp')]
  transfers between devices with their start and end apart: 7 -> 3, of which waited for: 3 -> 1; matrix products, arithmetic and copies ran while one was open for 23% -> 2% of each run, Pallas kernels for 0% -> 0%
where the time goes in v1:
time: 203 us; the launch traced here: 202 us
  blocking collectives  119 us (59%)
  Pallas kernels  49.8 us (25%)
  starting transfers between devices  9.71 us (5%)
  waiting for transfers between devices  9.4 us (5%)
  local copies, waits for them, and re-layouts  8.88 us (4%)
  other arithmetic  3.85 us (2%)
    all_gather x1, blocking collectives, body(): everyone = lax.all_gather(mine, 'seq')  45.2 us
    all_gather x1, blocking collectives, body(): filter_grad = lax.all_gather(reduced[2 * modes:], 'seq', axis=1)  38.6 us
    pallas_call x1, Pallas kernels, body(): pl.pallas_call(functools.partial(main_kernel, tokens, margin, modes, mode...  34.4 us
    all_to_all x2, blocking collectives, swap(): lax.all_to_all(blocks, 'seq', split_axis=0, concat_axis=0, tiled=True)  32.1 us
    pallas_call x1, Pallas kernels, body(): pl.pallas_call(functools.partial(ends_kernel, tokens, margin, modes), gri...  13.5 us
    all_to_all x1, waiting for transfers between devices, swap(): lax.all_to_all(blocks, 'seq', split_axis=0, concat_axis=0, tiled=True)  9.39 us
    ppermute x2, starting transfers between devices, passed_along(): return lax.ppermute(shard, axis, pairs)  6.14 us
  transfers between devices with their start and end apart: 3, of which 1 were waited for; matrix products, arithmetic and copies ran while one was open for 2% of the time, Pallas kernels for 0%

profile of v1, /device:TPU:0, one launch (start us, length us, event | category | flops | bytes accessed | tf_op | source)
XLA Modules:
  0.0 201.8 jit_solution(3383683536415033400)
XLA Ops:
  0.6 0.9 fusion.8
  1.5 1.0 fusion.6
  2.5 0.1 pad_maximum_fusion.2
  2.6 4.8 %collective-permute-start = (bf16[3,2,4096]{2,1,0:T(2,128)(2,1)S(1)}, bf16[3,2,4096]{2,1,0:T(2,128)(2,1)S(1)}, u32[]{:S(2)}, u32[]{:S(2)}) collective-permute-start(bf16[3,2,4096]{2,1,0:T(2,128)(2,1)S(1)} %pad_maximum_fusion.2), channel_id=1, source_target_pairs={{0,2},{2,4},{4,6},{6,8},{8,10},{10,12},{12,14},{14,16},{16,18},{18... | collective-permute-start | bytes 147464 | tf_op jit(solution)/shard_map/ppermute | solution.py:223
  7.5 0.9 slice.35
  8.3 0.0 copy-start.3
  8.3 0.1 pad_maximum_fusion.1
  8.5 1.3 collective-permute-start.1
  9.8 0.0 copy-done.3
  9.8 0.0 copy-start.4
  9.8 0.7 copy-done.4
  10.6 45.2 %all_gather.9 = f32[16,2,16,2,128]{4,3,0,2,1:T(2,128)S(1)} all-gather(f32[1,2,16,2,128]{4,3,0,2,1:T(2,128)S(1)} %pad_maximum_fusion.3), channel_id=1, replica_groups=mesh['seq'=16,'dp'=2] {'seq'}, dimensions={0}, use_global_device_ids=true | all-gather | bytes 557056 | tf_op jit(solution)/shard_map/all_gather | solution.py:243
  55.7 0.0 copy-start.1
  55.7 0.9 fusion.9
  56.6 0.1 copy-done.1
  56.8 0.8 reshape.53.taps
  57.5 0.0 collective-permute-done
  57.5 0.7 reshape.51.before
  58.2 0.0 collective-permute-done.1
  58.2 0.7 reshape.52.after
  58.9 13.5 %block_ends.1 = f32[16,1,2,32,128]{4,3,2,1,0:T(8,128)} custom-call(bf16[1,128,4096]{2,1,0:T(8,128)(2,1)} %q.3, bf16[1,128,4096]{2,1,0:T(8,128)(2,1)} %k.3, bf16[1,128,4096]{2,1,0:T(8,128)(2,1)} %v.3, bf16[1,128,4096]{2,1,0:T(8,128)(2,1)} %c.3, bf16[3,2,32,128]{3,2,1,0:T(8,128)(2,1)} %reshape.51.before, bf16[4,2,32,128]{3,2,1,0:T(8,128)(2,1)} %reshape.52.after, ...), custom_call_target="tpu_custom_call" | custom-call | tf_op jit(solution)/shard_map/block_ends/pallas_call | solution.py:269
  72.4 3.6 %all-to-all-start = ((f32[16,2,32,128]{3,2,1,0:T(8,128)}), f32[16,2,32,128]{3,2,1,0:T(8,128)S(1)}, u32[]{:S(2)}, u32[]{:S(2)}) async-start(f32[16,2,32,128]{3,2,1,0:T(8,128)} %bitcast.34), calls=%async_computation | async-start | bytes 1048576 | tf_op jit(solution)/shard_map/all_to_all | solution.py:217
  76.0 1.3 exponential_bitcast_fusion.power
  77.3 9.4 %all-to-all-done.got = f32[16,2,32,128]{3,2,1,0:T(8,128)S(1)} async-done(((f32[16,2,32,128]{3,2,1,0:T(8,128)}), f32[16,2,32,128]{3,2,1,0:T(8,128)S(1)}, u32[]{:S(2)}, u32[]{:S(2)}) %all-to-all-start) | async-done | bytes 524320 | tf_op jit(solution)/shard_map/all_to_all | solution.py:217
  86.7 0.0 copy-start
  86.7 0.8 copy-done
  87.5 1.9 carries.1
  89.4 15.0 %all_to_all.15 = f32[16,2,32,128]{3,2,1,0:T(8,128)} all-to-all(f32[16,2,32,128]{3,2,1,0:T(8,128)} %carries.1), channel_id=1, replica_groups=mesh['seq'=16,'dp'=2] {'seq'}, dimensions={0} | all-to-all | bytes 1048576 | tf_op jit(solution)/shard_map/all_to_all | solution.py:217
  104.4 34.4 %mixer.1 = (bf16[1,128,4096]{2,1,0:T(8,128)(2,1)}, bf16[1,128,4096]{2,1,0:T(8,128)(2,1)}, bf16[1,128,4096]{2,1,0:T(8,128)(2,1)}, f32[2,16,32,128]{3,2,1,0:T(8,128)}, f32[3,3,32,128]{3,2,1,0:T(8,128)}) custom-call(bf16[1,128,4096]{2,1,0:T(8,128)(2,1)} %q.3, bf16[1,128,4096]{2,1,0:T(8,128)(2,1)} %k.3, bf16[1,128,4096]{2,1,0:T(8,128)(2,1)} %v.3, ...), custom_call_target="tpu_custom_call" | custom-call | tf_op jit(solution)/shard_map/mixer/pallas_call | solution.py:291
  138.9 1.4 copy_bitcast_fusion
  140.3 17.1 %all_to_all.16 = f32[16,41,2,128]{3,2,1,0:T(2,128)S(1)} all-to-all(f32[16,41,2,128]{3,2,1,0:T(2,128)S(1)} %copy_bitcast_fusion), channel_id=1, replica_groups=mesh['seq'=16,'dp'=2] {'seq'}, dimensions={0} | all-to-all | bytes 1343488 | tf_op jit(solution)/shard_map/all_to_all | solution.py:217
  157.3 0.2 reduce_sum.9
  157.6 3.5 %psum.7 = f32[41,2,128]{2,1,0:T(2,128)S(1)} all-reduce(f32[41,2,128]{2,1,0:T(2,128)S(1)} %reduce_sum.9), channel_id=1, replica_groups=mesh['seq'=16,'dp'=2] {'dp'}, use_global_device_ids=true, to_apply=%region_1.2 | all-reduce | flops 10496 | bytes 83968 | tf_op jit(solution)/shard_map/psum | solution.py:313
  161.1 0.0 copy-start.2
  161.1 0.6 copy-done.2
  161.8 0.0 slice-start
  161.8 0.6 fusion.2
  162.4 0.0 slice-done
  162.5 38.6 %all-gather = f32[9,32,128]{2,0,1:T(8,128)S(1)} all-gather(f32[9,2,128]{2,0,1:T(8,128)S(1)} %copy.31), channel_id=2, replica_groups=mesh['seq'=16,'dp'=2] {'seq'}, dimensions={1}, use_global_device_ids=true | all-gather | bytes 156672 | tf_op jit(solution)/shard_map/all_gather | solution.py:316
  201.1 0.7 reshape.58
  (9 shorter events, 0.2 us)
Async XLA Ops:
  2.6 54.9 %collective-permute-start = (bf16[3,2,4096]{2,1,0:T(2,128)(2,1)S(1)}, bf16[3,2,4096]{2,1,0:T(2,128)(2,1)S(1)}, u32[]{:S(2)}, u32[]{:S(2)}) collective-permute-start(bf16[3,2,4096]{2,1,0:T(2,128)(2,1)S(1)} %pad_maximum_fusion.2), channel_id=1, source_target_pairs={{0,2},{2,4},{4,6},{6,8},{8,10},{10,12},{12,14},{14,16},{16,18},{18... | collective-permute-start | bytes 147464 | tf_op jit(solution)/shard_map/ppermute | solution.py:223
  8.3 1.4 copy-start.3
  8.5 49.7 %collective-permute-start.1 = (bf16[4,2,4096]{2,1,0:T(2,128)(2,1)S(1)}, bf16[4,2,4096]{2,1,0:T(2,128)(2,1)S(1)}, u32[]{:S(2)}, u32[]{:S(2)}) collective-permute-start(bf16[4,2,4096]{2,1,0:T(2,128)(2,1)S(1)} %pad_maximum_fusion.1), channel_id=1, source_target_pairs={{2,0},{4,2},{6,4},{8,6},{10,8},{12,10},{14,12},{16,14},{18,16},{20... | collective-permute-start | bytes 196616 | tf_op jit(solution)/shard_map/ppermute | solution.py:223
  9.8 0.7 copy-start.4
  55.7 1.0 copy-start.1
  72.4 14.3 %all-to-all-start = ((f32[16,2,32,128]{3,2,1,0:T(8,128)}), f32[16,2,32,128]{3,2,1,0:T(8,128)S(1)}, u32[]{:S(2)}, u32[]{:S(2)}) async-start(f32[16,2,32,128]{3,2,1,0:T(8,128)} %bitcast.34), calls=%async_computation | async-start | bytes 1048576 | tf_op jit(solution)/shard_map/all_to_all | solution.py:217
  86.7 0.8 copy-start
  161.1 0.6 copy-start.2
  161.8 0.7 slice-start

commit v2 on v1

--- a/solution.py
+++ b/solution.py
@@ -202,25 +202,146 @@
         gather_rows(source, target, tokens)
 
 
-def carry_kernel(count, power, got, out):
+MESH = pl.DeviceIdType.MESH
+
+
+def partner(d):
+    count = lax.axis_size("seq")
+    return lax.rem(lax.axis_index("seq") + d, count)
+
+
+def core_of():
+    return lax.rem(lax.axis_index("dp"), 2)
+
+
+def other_core():
+    return lax.axis_index("dp") + 1 - 2 * core_of()
+
+
+def greet():
+    count = lax.axis_size("seq")
+    barrier = pltpu.get_barrier_semaphore()
+    for d in range(1, count):
+        pl.semaphore_signal(barrier, inc=1, device_id={"seq": partner(d)}, device_id_type=MESH)
+    pl.semaphore_signal(barrier, inc=1, device_id={"dp": other_core()}, device_id_type=MESH)
+    pl.semaphore_wait(barrier, count)
+
+
+def remote(source, target, sems, d, device):
+    return pltpu.make_async_remote_copy(
+        src_ref=source,
+        dst_ref=target,
+        send_sem=sems.at[0, d],
+        recv_sem=sems.at[1, d],
+        device_id=device,
+        device_id_type=MESH,
+    )
+
+
+def to_all(source_of, target, sems):
+    me = lax.axis_index("seq")
+    copies = []
+    for d in range(1, lax.axis_size("seq")):
+        copy = remote(source_of(partner(d)), target.at[me], sems, d, {"seq": partner(d)})
+        copy.start()
+        copies.append(copy)
+    return copies
+
+
+def wait_all(copies):
+    for copy in copies:
+        copy.wait()
+
+
+def start_kernel(
+    mine, before, after, everyone, got_before, got_after, slots, left, right, sems, halo_sems, swap_sems
+):
+    me = lax.axis_index("seq")
+    count = lax.axis_size("seq")
+    core = core_of()
+    greet()
+    halos = [
+        remote(before, left, halo_sems, 0, {"seq": partner(1)}),
+        remote(after, right, halo_sems, 1, {"seq": partner(count - 1)}),
+    ]
+    for copy in halos:
+        copy.start()
+    copies = to_all(lambda p: mine.at[core], slots.at[core], sems)
+    slots[core, me] = mine[core]
+    wait_all(copies)
+    copy = remote(slots.at[core], slots.at[core], swap_sems, 0, {"dp": other_core()})
+    copy.start()
+    wait_all(halos)
+    got_before[...] = jnp.where(me > 0, left[...].astype(F32), 0.0).astype(BF16)
+    got_after[...] = jnp.where(me < count - 1, right[...].astype(F32), 0.0).astype(BF16)
+    copy.wait()
+    everyone[...] = slots[...]
+
+
+def carry_kernel(state, power, out, got, sent, landed, out_sems, back_sems):
+    me = lax.axis_index("seq")
+    count = lax.axis_size("seq")
+    greet()
+    copies = to_all(lambda p: state.at[p], got, out_sems)
+    got[me] = state[me]
     factor = power[...]
     ahead = jnp.zeros_like(factor)
     back = jnp.zeros_like(factor)
+    wait_all(copies)
     for p in range(count):
-        out[p, 0] = ahead
+        sent[p, 0] = ahead
         ahead = factor * ahead + got[p, 0]
-        out[count - 1 - p, 1] = back
+        sent[count - 1 - p, 1] = back
         back = factor * back + got[count - 1 - p, 1]
-
-
-def swap(blocks):
-    return lax.all_to_all(blocks, "seq", split_axis=0, concat_axis=0, tiled=True)
-
-
-def passed_along(shard, axis, by):
-    count = lax.axis_size(axis)
-    pairs = [(i, i + by) for i in range(count) if 0 <= i + by < count]
-    return lax.ppermute(shard, axis, pairs)
+    copies = to_all(lambda p: sent.at[p], landed, back_sems)
+    landed[me] = sent[me]
+    wait_all(copies)
+    out[...] = landed[...]
+
+
+def reduce_kernel(packed, out, other, summed, got, sems, swap_sems):
+    me = lax.axis_index("seq")
+    core = core_of()
+    greet()
+    copy = remote(packed.at[1 - core], other, swap_sems, 0, {"dp": other_core()})
+    copy.start()
+    copy.wait()
+    summed[...] = packed[core] + other[...]
+    copies = to_all(lambda p: summed.at[p], got, sems)
+    got[me] = summed[me]
+    wait_all(copies)
+    total = got[0]
+    for p in range(1, got.shape[0]):
+        total = total + got[p]
+    out[...] = total
+
+
+def share_kernel(start, half, out, taps, both, slots, sems, swap_sems):
+    me = lax.axis_index("seq")
+    core = core_of()
+    greet()
+    both[core] = half[...]
+    copy = remote(both.at[core], both.at[core], swap_sems, 0, {"dp": other_core()})
+    copy.start()
+    copy.wait()
+    rows = both.at[1, pl.ds(start, slots.shape[1])]
+    copies = to_all(lambda p: rows, slots, sems)
+    slots[me] = both[1, pl.ds(start, slots.shape[1])]
+    wait_all(copies)
+    out[...] = both[...]
+    taps[...] = slots[...]
+
+
+def comm_call(kernel, ident, name, shapes, scratch):
+    return pl.pallas_call(
+        kernel,
+        out_shape=shapes,
+        scratch_shapes=scratch,
+        compiler_params=pltpu.CompilerParams(
+            collective_id=ident, has_side_effects=True, vmem_limit_bytes=32 << 20
+        ),
+        name=name,
+    )
 
 
 def body(query_rows, key_rows, value_rows, cotangent, short_filter, residue, decay_rate):
@@ -239,15 +360,34 @@
     vmem = 56 << 20
 
     root = jnp.sqrt(-jnp.expm1(-2.0 * decay_rate))
-    mine = jnp.stack([decay_rate.T, (residue * root).T]).reshape(2, modes, own, LANES)
-    everyone = lax.all_gather(mine, "seq")
-    rate, weight = everyone.transpose(1, 2, 0, 3, 4).reshape(2, modes, tiles, LANES)
-
+    both = pltpu.SemaphoreType.DMA((2, count))
+    pair = pltpu.SemaphoreType.DMA((2, 2))
+    mine = jnp.stack([decay_rate.T, (residue * root).T]).reshape(2, modes * own, LANES)
     rows = (query_rows, key_rows, value_rows, cotangent)
     before = jnp.stack([x[0, tokens - margin :] for x in rows[:3]])
-    before = passed_along(before, "seq", 1).reshape(3, margin, tiles, LANES)
-    after = jnp.stack([x[0, :margin] for x in rows])
-    after = passed_along(after, "seq", -1).reshape(4, margin, tiles, LANES)
+    before = before.reshape(3, margin, tiles, LANES)
+    after = jnp.stack([x[0, :margin] for x in rows]).reshape(4, margin, tiles, LANES)
+    slots = (2, count, modes * own, LANES)
+    everyone, before, after = comm_call(
+        start_kernel,
+        0,
+        "gather_modes",
+        [
+            jax.ShapeDtypeStruct(slots, F32),
+            jax.ShapeDtypeStruct(before.shape, BF16),
+            jax.ShapeDtypeStruct(after.shape, BF16),
+        ],
+        [
+            pltpu.VMEM(slots, F32),
+            pltpu.VMEM(before.shape, BF16),
+            pltpu.VMEM(after.shape, BF16),
+            both,
+            pair,
+            pair,
+        ],
+    )(mine, before, after)
+    everyone = everyone.reshape(2, count, modes, own, LANES)
+    rate, weight = everyone.transpose(0, 2, 1, 3, 4).reshape(2, modes, tiles, LANES)
     taps = short_filter.reshape(3, margin + 1, tiles, LANES)
 
     rows_spec = pl.BlockSpec((1, tokens, WIDE), lambda i: (0, 0, i))
@@ -277,15 +417,16 @@
         name="block_ends",
     )(*rows, before, after, taps, rate)
 
-    got = swap(state.reshape(count, 2, tiles // split, LANES))
     slices = rate.reshape(count, tiles // split, LANES)
     power = jnp.exp(-tokens * lax.dynamic_index_in_dim(slices, lax.axis_index("seq"), 0, False))
-    carried = pl.pallas_call(
-        functools.partial(carry_kernel, count),
-        out_shape=jax.ShapeDtypeStruct(got.shape, F32),
-        name="carries",
-    )(power, got)
-    state = swap(carried).reshape(state.shape)
+    blocked = (count, 2, tiles // split, LANES)
+    state = comm_call(
+        carry_kernel,
+        1,
+        "carry_states",
+        jax.ShapeDtypeStruct(blocked, F32),
+        [pltpu.VMEM(blocked, F32)] * 3 + [both] * 2,
+    )(state.reshape(blocked), power).reshape(state.shape)
 
     shapes = [jax.ShapeDtypeStruct(query_rows.shape, BF16)] * 3
     dq, dk, dv, sums, tap_sums = pl.pallas_call(
@@ -306,17 +447,45 @@
         name="mixer",
     )(*rows, before, after, taps, rate, weight, state)
 
-    terms = 2 * modes + 3 * (margin + 1)
+    terms = (2 * modes + 3 * (margin + 1)) * own
+    sum_rows = 2 * modes * own
+    padded = -(-terms // 16) * 16
+    half = padded // 2
     packed = jnp.concatenate(
         [sums.reshape(2 * modes, count, own, LANES), tap_sums.reshape(-1, count, own, LANES)]
-    ).transpose(1, 0, 2, 3)
-    reduced = lax.psum(jnp.sum(swap(packed), axis=0), "dp")
-    factor = 1.0 / math.sqrt(batch * lax.axis_size("dp") * length)
-    reduced = reduced * factor
-    filter_grad = lax.all_gather(reduced[2 * modes :], "seq", axis=1)
+    )
+    packed = packed.transpose(1, 0, 2, 3).reshape(count, terms, LANES)
+    packed = jnp.pad(packed, ((0, 0), (0, padded - terms), (0, 0)))
+    packed = packed.reshape(count, 2, half, LANES).transpose(1, 0, 2, 3)
+    blocked = (count, half, LANES)
+    reduced = comm_call(
+        reduce_kernel,
+        2,
+        "reduce_sums",
+        jax.ShapeDtypeStruct((half, LANES), F32),
+        [pltpu.VMEM(blocked, F32)] * 3 + [both, pair],
+    )(packed)
+    cores = lax.axis_size("dp")
+    if cores > 2:
+        groups = [[j for j in range(cores) if j % 2 == i] for i in range(2)]
+        reduced = lax.psum(reduced, "dp", axis_index_groups=groups)
+    tap_start = sum_rows - half
+    tap_rows = padded - sum_rows
+    slots = (count, tap_rows, LANES)
+    reduced, filter_grad = comm_call(
+        functools.partial(share_kernel, tap_start),
+        3,
+        "share_taps",
+        [jax.ShapeDtypeStruct((2, half, LANES), F32), jax.ShapeDtypeStruct(slots, F32)],
+        [pltpu.VMEM((2, half, LANES), F32), pltpu.VMEM(slots, F32), both, pair],
+    )(reduced)
+    factor = 1.0 / math.sqrt(batch * cores * length)
+    reduced = reduced.reshape(padded, LANES)[:sum_rows] * factor
+    filter_grad = filter_grad[:, : terms - sum_rows] * factor
+    filter_grad = filter_grad.reshape(count, 3, margin + 1, own * LANES).transpose(1, 2, 0, 3)
     filter_grad = filter_grad.reshape(3, margin + 1, width)
     first_sum, second_sum = (
-        reduced[: 2 * modes].reshape(2, modes, own * LANES).transpose(0, 2, 1)
+        reduced.reshape(2, modes, own * LANES).transpose(0, 2, 1)
     )
     residue_grad = root * first_sum
     rate_grad = (

time: 203 us -> 137 us (0.67)
  blocking collectives: 119 us -> 0 us
  Pallas kernels: 49.8 us -> 122 us
  starting transfers between devices: 9.71 us -> 0 us
  waiting for transfers between devices: 9.4 us -> 0 us
  local copies, waits for them, and re-layouts: 8.88 us -> 12.2 us
  other arithmetic: 3.85 us -> 0.94 us
    all_gather x2 -> x0, blocking collectives: 83.7 us -> none  [the longest x1 45.2 us: body(): everyone = lax.all_gather(mine, 'seq')]
    pallas_call x1 -> x4, Pallas kernels: 1.89 us -> 74.4 us  [the longest x1 28.1 us: body(): comm_call(carry_kernel, 1, 'carry_states', jax.ShapeDtypeStruct(blocked,...]
    all_to_all x2 -> x0, blocking collectives: 32.1 us -> none  [swap(): lax.all_to_all(blocks, 'seq', split_axis=0, concat_axis=0, tiled=True)]
    all_to_all x1 -> x0, waiting for transfers between devices: 9.39 us -> none  [swap(): lax.all_to_all(blocks, 'seq', split_axis=0, concat_axis=0, tiled=True)]
    ppermute x2 -> x0, starting transfers between devices: 6.14 us -> none  [passed_along(): return lax.ppermute(shard, axis, pairs)]
    all_to_all x1 -> x0, starting transfers between devices: 3.57 us -> none  [swap(): lax.all_to_all(blocks, 'seq', split_axis=0, concat_axis=0, tiled=True)]
    psum x1 -> x0, blocking collectives: 3.52 us -> none  [body(): reduced = lax.psum(jnp.sum(swap(packed), axis=0), 'dp')]
  transfers between devices with their start and end apart: 3 -> 0, of which waited for: 1 -> 0; matrix products, arithmetic and copies ran while one was open for 2% -> 0% of each run, Pallas kernels for 0% -> 0%
where the time goes in v2:
time: 137 us; the launch traced here: 136 us
  Pallas kernels  122 us (89%)
  local copies, waits for them, and re-layouts  12.2 us (9%)
    pallas_call x1, Pallas kernels, body(): pl.pallas_call(functools.partial(main_kernel, tokens, margin, modes, mode...  34.4 us
    pallas_call x1, Pallas kernels, body(): comm_call(carry_kernel, 1, 'carry_states', jax.ShapeDtypeStruct(blocked,...  28.1 us
    pallas_call x1, Pallas kernels, body(): comm_call(reduce_kernel, 2, 'reduce_sums', jax.ShapeDtypeStruct((half, LA...  17.6 us
    pallas_call x1, Pallas kernels, body(): comm_call(start_kernel, 0, 'gather_modes', [jax.ShapeDtypeStruct(slots, F...  14.9 us
    pallas_call x1, Pallas kernels, body(): comm_call(functools.partial(share_kernel, tap_start), 3, 'share_taps', [j...  13.7 us
    pallas_call x1, Pallas kernels, body(): pl.pallas_call(functools.partial(ends_kernel, tokens, margin, modes), gri...  13.5 us
    unnamed x16, local copies, waits for them, and re-layouts  3.62 us
    slice x3, local copies, waits for them, and re-layouts, body(): x[0, :margin]  2.75 us

profile of v2, /device:TPU:0, one launch (start us, length us, event | category | flops | bytes accessed | tf_op | source)
XLA Modules:
  0.0 136.3 jit_solution(12109253766825791)
XLA Ops:
  0.6 0.0 copy-start.6
  0.6 0.0 copy-start.7
  0.7 0.8 stack.15
  1.4 0.0 copy-done.6
  1.4 0.0 copy-done.7
  1.5 0.9 slice.35
  2.3 0.9 fusion.8
  3.2 1.0 fusion.6
  4.2 0.1 pad_maximum_fusion.1
  4.4 0.0 copy-start.5
  4.4 0.1 reshape.68.after
  4.4 0.1 pad_maximum_fusion.2
  4.6 0.7 copy-done.5
  5.3 0.8 reshape.69.taps
  6.1 14.9 %gather_modes.1 = (f32[2,16,32,128]{3,2,1,0:T(8,128)S(1)}, bf16[3,2,32,128]{3,2,1,0:T(8,128)(2,1)S(1)}, bf16[4,2,32,128]{3,2,1,0:T(8,128)(2,1)S(1)}) custom-call(f32[2,32,128]{2,1,0:T(8,128)S(1)} %pad_maximum_fusion.3.mine, bf16[3,2,32,128]{3,2,1,0:T(8,128)(2,1)S(1)} %reshape.67.before, bf16[4,2,32,128]{3,2,1,0:T(8,128)(2,1)S(1)} %reshape.68.after), custom_call_target="tpu_custom_call" | custom-call | tf_op jit(solution)/shard_map/gather_modes/pallas_call | solution.py:371
  20.9 0.0 copy-start.2
  21.0 0.0 copy-start.3
  21.0 0.3 copy.31
  21.2 0.3 copy-done.2
  21.6 0.0 copy-done.3
  21.6 0.8 fusion.9
  22.4 0.0 copy-start.4
  22.4 0.7 copy-done.4
  23.1 13.5 %block_ends.1 = f32[16,1,2,32,128]{4,3,2,1,0:T(8,128)} custom-call(bf16[1,128,4096]{2,1,0:T(8,128)(2,1)} %q.3, bf16[1,128,4096]{2,1,0:T(8,128)(2,1)} %k.3, bf16[1,128,4096]{2,1,0:T(8,128)(2,1)} %v.3, bf16[1,128,4096]{2,1,0:T(8,128)(2,1)} %c.3, bf16[3,2,32,128]{3,2,1,0:T(8,128)(2,1)} %copy-done.3, bf16[4,2,32,128]{3,2,1,0:T(8,128)(2,1)} %copy-done.2, ...), custom_call_target="tpu_custom_call" | custom-call | tf_op jit(solution)/shard_map/block_ends/pallas_call | solution.py:409
  36.6 0.0 copy-start
  36.6 1.0 copy-done
  37.7 28.1 %carry_states.1 = f32[16,2,32,128]{3,2,1,0:T(8,128)S(1)} custom-call(f32[16,2,32,128]{3,2,1,0:T(8,128)S(1)} %bitcast.42, f32[32,128]{1,0:T(8,128)S(1)} %exponential_bitcast_fusion.power), custom_call_target="tpu_custom_call" | custom-call | tf_op jit(solution)/shard_map/carry_states/pallas_call | solution.py:423
  65.8 0.0 copy-start.1
  65.8 0.8 copy-done.1
  66.6 34.4 %mixer.1 = (bf16[1,128,4096]{2,1,0:T(8,128)(2,1)}, bf16[1,128,4096]{2,1,0:T(8,128)(2,1)}, bf16[1,128,4096]{2,1,0:T(8,128)(2,1)}, f32[2,16,32,128]{3,2,1,0:T(8,128)}, f32[3,3,32,128]{3,2,1,0:T(8,128)}) custom-call(bf16[1,128,4096]{2,1,0:T(8,128)(2,1)} %q.3, bf16[1,128,4096]{2,1,0:T(8,128)(2,1)} %k.3, bf16[1,128,4096]{2,1,0:T(8,128)(2,1)} %v.3, ...), custom_call_target="tpu_custom_call" | custom-call | tf_op jit(solution)/shard_map/mixer/pallas_call | solution.py:432
  101.0 0.9 copy.22
  101.9 1.1 copy.21
  103.1 0.1 pad.4
  103.1 0.2 copy.30
  103.4 17.6 %reduce_sums.1.half = f32[48,128]{1,0:T(8,128)S(1)} custom-call(f32[2,16,48,128]{3,2,1,0:T(8,128)S(1)} %bitcast.41), custom_call_target="tpu_custom_call" | custom-call | tf_op jit(solution)/shard_map/reduce_sums/pallas_call | solution.py:461
  121.0 13.7 %share_taps.1 = (f32[2,48,128]{2,1,0:T(8,128)S(1)}, f32[16,32,128]{2,1,0:T(8,128)S(1)}) custom-call(f32[48,128]{1,0:T(8,128)S(1)} %reduce_sums.1.half), custom_call_target="tpu_custom_call" | custom-call | tf_op jit(solution)/shard_map/share_taps/pallas_call | solution.py:475
  134.8 0.1 reshape.77
  134.9 0.6 fusion.2
  135.6 0.8 reshape.78
  (10 shorter events, 0.2 us)
Async XLA Ops:
  0.6 0.8 copy-start.6
  0.6 0.8 copy-start.7
  4.4 0.9 copy-start.5
  20.9 0.6 copy-start.2
  21.0 0.6 copy-start.3
  22.4 0.7 copy-start.4
  36.6 1.0 copy-start
  65.8 0.8 copy-start.1

commit v3 on v1

--- a/solution.py
+++ b/solution.py
@@ -26,11 +26,11 @@
     return values.astype(BF16).astype(F32)
 
 
-def spread_rows(source, target, shift, tokens):
+def spread_rows(source, target, shift, tokens, base=0):
     def step(i, carry):
         start = pl.multiple_of(i * 16, 16)
         for s in range(GROUPS):
-            piece = source[0, pl.ds(start, 16), s * LANES : (s + 1) * LANES].astype(F32)
+            piece = source[0, pl.ds(start, 16), pl.ds(base + s * LANES, LANES)].astype(F32)
             target[pl.ds((start + shift) * GROUPS + s, 16, stride=GROUPS), :] = piece
         return carry
 
@@ -77,28 +77,6 @@
     lax.fori_loop(0, tokens + margin, step, 0, unroll=2)
 
 
-def ends_kernel(tokens, margin, modes, q, k, v, c, before, after, taps, rate, state, w0, w1, w2, w3, gated, grad_mixed):
-    wide = (w0, w1, w2, w3)
-    load_inputs(tokens, margin, (q, k, v, c), before, after, wide)
-    short_products(tokens, margin, taps, wide, gated, grad_mixed, None)
-    decay = [jnp.exp(-rate[n]) for n in range(modes)]
-    zero = jnp.zeros((GROUPS, LANES), F32)
-
-    def step(t, carry):
-        ahead, back = carry
-        u = gated[row(t), :]
-        g = grad_mixed[row(tokens - 1 - t), :]
-        return (
-            tuple(decay[n] * ahead[n] + u for n in range(modes)),
-            tuple(decay[n] * back[n] + g for n in range(modes)),
-        )
-
-    ahead, back = lax.fori_loop(0, tokens, step, ((zero,) * modes, (zero,) * modes), unroll=2)
-    for n in range(modes):
-        state[n, 0, 0] = ahead[n]
-        state[n, 0, 1] = back[n]
-
-
 def main_kernel(
     tokens, margin, modes, part, q, k, v, c, before, after, taps, rate, weight, state,
     dq, dk, dv, sums, tap_sums,
@@ -132,7 +110,7 @@
             mixed[row(t), :] = y
             return (x, tuple(dots[n] + g * x[n] for n in range(part)))
 
-        start = tuple(state[n, 0, 0] for n in some)
+        start = tuple(state[0, n, 0] for n in some)
         x, dots = lax.fori_loop(0, tokens, forward, (start, (zero,) * part), unroll=2)
         for n in range(part):
             sums[0, first + n] = dots[n]
@@ -156,7 +134,7 @@
             grad_gated[row(t), :] = y
             return (h, dots)
 
-        start = tuple(state[n, 0, 1] for n in some)
+        start = tuple(state[0, n, 1] for n in some)
         h, dots = lax.fori_loop(0, tokens, backward, (start, (zero,) * part), unroll=2)
         for n in range(part):
             sums[1, first + n] = decay[n] * dots[n]
@@ -202,25 +180,240 @@
         gather_rows(source, target, tokens)
 
 
-def carry_kernel(count, power, got, out):
-    factor = power[...]
-    ahead = jnp.zeros_like(factor)
-    back = jnp.zeros_like(factor)
-    for p in range(count):
-        out[p, 0] = ahead
-        ahead = factor * ahead + got[p, 0]
-        out[count - 1 - p, 1] = back
-        back = factor * back + got[count - 1 - p, 1]
-
-
-def swap(blocks):
-    return lax.all_to_all(blocks, "seq", split_axis=0, concat_axis=0, tiled=True)
-
-
-def passed_along(shard, axis, by):
-    count = lax.axis_size(axis)
-    pairs = [(i, i + by) for i in range(count) if 0 <= i + by < count]
-    return lax.ppermute(shard, axis, pairs)
+MESH = pl.DeviceIdType.MESH
+
+
+def partner(d):
+    count = lax.axis_size("seq")
+    return lax.rem(lax.axis_index("seq") + d, count)
+
+
+def core_of():
+    return lax.rem(lax.axis_index("dp"), 2)
+
+
+def other_core():
+    return lax.axis_index("dp") + 1 - 2 * core_of()
+
+
+def greet():
+    count = lax.axis_size("seq")
+    barrier = pltpu.get_barrier_semaphore()
+
+    def step(d, carry):
+        pl.semaphore_signal(barrier, inc=1, device_id={"seq": partner(d)}, device_id_type=MESH)
+        return carry
+
+    lax.fori_loop(1, count, step, 0)
+    pl.semaphore_signal(barrier, inc=1, device_id={"dp": other_core()}, device_id_type=MESH)
+    pl.semaphore_wait(barrier, count)
+
+
+def remote(source, target, sems, d, device):
+    return pltpu.make_async_remote_copy(
+        src_ref=source,
+        dst_ref=target,
+        send_sem=sems.at[0, d],
+        recv_sem=sems.at[1, d],
+        device_id=device,
+        device_id_type=MESH,
+    )
+
+
+class ToAll:
+
+    def __init__(self, source_of, target, sems):
+        self.source_of, self.target, self.sems = source_of, target, sems
+
+    def copy(self, d):
+        p = partner(d)
+        slot = self.target.at[lax.axis_index("seq")]
+        return remote(self.source_of(p), slot, self.sems, d, {"seq": p})
+
+    def start(self):
+        def step(d, carry):
+            self.copy(d).start()
+            return carry
+
+        lax.fori_loop(1, lax.axis_size("seq"), step, 0)
+
+    def wait(self):
+        def step(d, carry):
+            self.copy(d).wait()
+            return carry
+
+        lax.fori_loop(1, lax.axis_size("seq"), step, 0)
+
+
+def to_other_core(ref, sems, d):
+    return remote(ref, ref, sems, d, {"dp": other_core()})
+
+
+def front_kernel(
+    tokens, margin, modes, blocks, own,
+    q, k, v, c, mine, before, after, taps,
+    modal, got_before, got_after, carried,
+    w0, w1, w2, w3, gated, grad_mixed, slots, table, left, right, state, got, sent, landed,
+    slot_sems, halo_sems, swap_sems, out_sems, back_sems,
+):
+    me = lax.axis_index("seq")
+    count = lax.axis_size("seq")
+    core = core_of()
+    units = 2 * modes // count
+    wide = (w0, w1, w2, w3)
+    greet()
+    halos = [
+        remote(before, left, halo_sems, 0, {"seq": partner(1)}),
+        remote(after, right, halo_sems, 1, {"seq": partner(count - 1)}),
+    ]
+    for copy in halos:
+        copy.start()
+    gathering = ToAll(lambda p: mine.at[core], slots.at[core], slot_sems)
+    gathering.start()
+    slots[core, me] = mine[core]
+    for b in range(blocks):
+        for i, x in enumerate((q, k, v, c)):
+            spread_rows(x, wide[i].at[b], margin, tokens, b * WIDE)
+    gathering.wait()
+    copy = to_other_core(slots.at[core], swap_sems, 0)
+    copy.start()
+    for halo in halos:
+        halo.wait()
+    got_before[...] = jnp.where(me > 0, left[...].astype(F32), 0.0).astype(BF16)
+    got_after[...] = jnp.where(me < count - 1, right[...].astype(F32), 0.0).astype(BF16)
+    copy.wait()
+
+    def arrange(n, carry):
+        for i in range(2):
+            for p in range(count):
+                table[i, n, p * own : (p + 1) * own, :] = slots[i, p, n]
+        return carry
+
+    lax.fori_loop(0, modes, arrange, 0)
+    modal[...] = table[...]
+    zero = jnp.zeros((GROUPS, LANES), F32)
+
+    def out_copies(b):
+        return ToAll(lambda p: state.at[b, p], got.at[b], out_sems.at[b])
+
+    def back_copies(b):
+        return ToAll(lambda p: sent.at[b, p], landed.at[b], back_sems.at[b])
+
+    def combine(b):
+        out_copies(b).wait()
+        cols = slice(b * GROUPS, (b + 1) * GROUPS)
+        for unit in range(units):
+            which = me * units + unit
+            backward = lax.rem(which, 2)
+            factor = jnp.exp(-tokens * table[0, lax.div(which, 2), cols, :])
+
+            def step(p, total):
+                place = p + backward * (count - 1 - 2 * p)
+                sent[b, place, unit] = total
+                return factor * total + got[b, place, unit]
+
+            lax.fori_loop(0, count, step, zero, unroll=4)
+        back_copies(b).start()
+        landed[b, me] = sent[b, me]
+
+    for b in range(blocks):
+        cols = slice(b * GROUPS, (b + 1) * GROUPS)
+        mine_wide = [x.at[b] for x in wide]
+        for i in range(4):
+            for j in range(margin):
+                if i < 3:
+                    mine_wide[i][row(j), :] = got_before[i, j, cols, :].astype(F32)
+                mine_wide[i][row(margin + tokens + j), :] = got_after[i, j, cols, :].astype(F32)
+        short_products(tokens, margin, taps[:, :, cols, :], mine_wide, gated, grad_mixed, None)
+        decay = [jnp.exp(-table[0, n, cols, :]) for n in range(modes)]
+
+        def step(t, carry):
+            ahead, back = carry
+            u = gated[row(t), :]
+            g = grad_mixed[row(tokens - 1 - t), :]
+            return (
+                tuple(decay[n] * ahead[n] + u for n in range(modes)),
+                tuple(decay[n] * back[n] + g for n in range(modes)),
+            )
+
+        ends = lax.fori_loop(0, tokens, step, ((zero,) * modes, (zero,) * modes), unroll=2)
+        for n in range(modes):
+            for i in range(2):
+                unit = 2 * n + i
+                state[b, unit // units, unit % units] = ends[i][n]
+        out_copies(b).start()
+        got[b, me] = state[b, me]
+        if b > 0:
+            combine(b - 1)
+    combine(blocks - 1)
+    for b in range(blocks):
+        back_copies(b).wait()
+    carried[...] = landed[...]
+
+
+def reduce_part(packed, other, summed, got, sems, swap_sems):
+    me = lax.axis_index("seq")
+    core = core_of()
+    copy = remote(packed.at[1 - core], other, swap_sems, 0, {"dp": other_core()})
+    copy.start()
+    copy.wait()
+    summed[...] = packed[core] + other[...]
+    copies = ToAll(lambda p: summed.at[p], got, sems)
+    copies.start()
+    got[me] = summed[me]
+    copies.wait()
+    total = got[0]
+    for p in range(1, got.shape[0]):
+        total = total + got[p]
+    return total
+
+
+def share_part(total, sums, taps, both, slots, sems, swap_sems):
+    me = lax.axis_index("seq")
+    core = core_of()
+    count, tap_rows = slots.shape[1:3]
+    sum_rows = total.shape[0] - tap_rows
+    both[core] = total[:sum_rows]
+    slots[core, me] = total[sum_rows:]
+    copies = ToAll(lambda p: slots.at[core, me], slots.at[core], sems)
+    copies.start()
+    first = to_other_core(both.at[core], swap_sems, 1)
+    first.start()
+    copies.wait()
+    second = to_other_core(slots.at[core], swap_sems, 2)
+    second.start()
+    first.wait()
+    second.wait()
+    sums[...] = both[...]
+    taps[...] = slots[...]
+
+
+def reduce_kernel(packed, out, other, summed, got, sems, swap_sems):
+    greet()
+    out[...] = reduce_part(packed, other, summed, got, sems, swap_sems)
+
+
+def share_kernel(half, sums, taps, both, slots, sems, swap_sems):
+    greet()
+    share_part(half[...], sums, taps, both, slots, sems, swap_sems)
+
+
+def end_kernel(packed, sums, taps, other, summed, got, both, slots, sems, share_sems, swap_sems):
+    greet()
+    total = reduce_part(packed, other, summed, got, sems, swap_sems)
+    share_part(total, sums, taps, both, slots, share_sems, swap_sems)
+
+
+def comm_call(kernel, ident, name, shapes, scratch):
+    return pl.pallas_call(
+        kernel,
+        out_shape=shapes,
+        scratch_shapes=scratch,
+        compiler_params=pltpu.CompilerParams(
+            collective_id=ident, has_side_effects=True, vmem_limit_bytes=56 << 20
+        ),
+        name=name,
+    )
 
 
 def body(query_rows, key_rows, value_rows, cotangent, short_filter, residue, decay_rate):
@@ -231,24 +424,53 @@
     count = lax.axis_size("seq")
     own = residue.shape[0] // LANES
     tiles = width // LANES
-    split = count // modes
-    assert split * modes == count
-    per = tiles // split // GROUPS
     blocks = width // WIDE
+    assert 2 * modes % count == 0
+    units = 2 * modes // count
     length = tokens * count
     vmem = 56 << 20
 
     root = jnp.sqrt(-jnp.expm1(-2.0 * decay_rate))
+    each = pltpu.SemaphoreType.DMA((2, count))
+    each_block = pltpu.SemaphoreType.DMA((blocks, 2, count))
+    few = pltpu.SemaphoreType.DMA((2, 3))
     mine = jnp.stack([decay_rate.T, (residue * root).T]).reshape(2, modes, own, LANES)
-    everyone = lax.all_gather(mine, "seq")
-    rate, weight = everyone.transpose(1, 2, 0, 3, 4).reshape(2, modes, tiles, LANES)
-
     rows = (query_rows, key_rows, value_rows, cotangent)
     before = jnp.stack([x[0, tokens - margin :] for x in rows[:3]])
-    before = passed_along(before, "seq", 1).reshape(3, margin, tiles, LANES)
-    after = jnp.stack([x[0, :margin] for x in rows])
-    after = passed_along(after, "seq", -1).reshape(4, margin, tiles, LANES)
+    before = before.reshape(3, margin, tiles, LANES)
+    after = jnp.stack([x[0, :margin] for x in rows]).reshape(4, margin, tiles, LANES)
     taps = short_filter.reshape(3, margin + 1, tiles, LANES)
+
+    def scratch(n, *lead):
+        return pltpu.VMEM(lead + (n * GROUPS, LANES), F32)
+
+    def vmem_like(shape):
+        return pltpu.VMEM(shape, F32)
+
+    moving = (blocks, count, units, GROUPS, LANES)
+    modal, before, after, state = comm_call(
+        functools.partial(front_kernel, tokens, margin, modes, blocks, own),
+        0,
+        "block_states",
+        [
+            jax.ShapeDtypeStruct((2, modes, tiles, LANES), F32),
+            jax.ShapeDtypeStruct(before.shape, BF16),
+            jax.ShapeDtypeStruct(after.shape, BF16),
+            jax.ShapeDtypeStruct(moving, F32),
+        ],
+        [scratch(tokens + 2 * margin, blocks)] * 4
+        + [scratch(tokens + margin)] * 2
+        + [
+            vmem_like((2, count, modes, own, LANES)),
+            vmem_like((2, modes, tiles, LANES)),
+            pltpu.VMEM(before.shape, BF16),
+            pltpu.VMEM(after.shape, BF16),
+        ]
+        + [vmem_like(moving)] * 4
+        + [each, few, few, each_block, each_block],
+    )(*rows, mine, before, after, taps)
+    rate, weight = modal
+    state = state.reshape(blocks, modes, 2, GROUPS, LANES)
 
     rows_spec = pl.BlockSpec((1, tokens, WIDE), lambda i: (0, 0, i))
 
@@ -256,37 +478,10 @@
         zeros = (0,) * len(lead)
         return pl.BlockSpec(lead + (GROUPS, LANES), lambda i: zeros + (i, 0))
 
-    state_spec = pl.BlockSpec(
-        (modes, 1, 2, GROUPS, LANES), lambda i: (0, i // per, 0, i % per, 0)
-    )
-
-    def scratch(n):
-        return pltpu.VMEM((n * GROUPS, LANES), F32)
-
+    state_spec = pl.BlockSpec((1, modes, 2, GROUPS, LANES), lambda i: (i, 0, 0, 0, 0))
     params = pltpu.CompilerParams(vmem_limit_bytes=vmem)
     head = [rows_spec] * 4 + [tile_spec(3, margin), tile_spec(4, margin), tile_spec(3, margin + 1), tile_spec(modes)]
     wide = [scratch(tokens + 2 * margin)] * 4
-    state = pl.pallas_call(
-        functools.partial(ends_kernel, tokens, margin, modes),
-        grid=(blocks,),
-        in_specs=head,
-        out_specs=state_spec,
-        out_shape=jax.ShapeDtypeStruct((modes, split, 2, tiles // split, LANES), F32),
-        scratch_shapes=wide + [scratch(tokens + margin)] * 2,
-        compiler_params=params,
-        name="block_ends",
-    )(*rows, before, after, taps, rate)
-
-    got = swap(state.reshape(count, 2, tiles // split, LANES))
-    slices = rate.reshape(count, tiles // split, LANES)
-    power = jnp.exp(-tokens * lax.dynamic_index_in_dim(slices, lax.axis_index("seq"), 0, False))
-    carried = pl.pallas_call(
-        functools.partial(carry_kernel, count),
-        out_shape=jax.ShapeDtypeStruct(got.shape, F32),
-        name="carries",
-    )(power, got)
-    state = swap(carried).reshape(state.shape)
-
     shapes = [jax.ShapeDtypeStruct(query_rows.shape, BF16)] * 3
     dq, dk, dv, sums, tap_sums = pl.pallas_call(
         functools.partial(main_kernel, tokens, margin, modes, modes // 2),
@@ -306,17 +501,46 @@
         name="mixer",
     )(*rows, before, after, taps, rate, weight, state)
 
-    terms = 2 * modes + 3 * (margin + 1)
-    packed = jnp.concatenate(
-        [sums.reshape(2 * modes, count, own, LANES), tap_sums.reshape(-1, count, own, LANES)]
-    ).transpose(1, 0, 2, 3)
-    reduced = lax.psum(jnp.sum(swap(packed), axis=0), "dp")
-    factor = 1.0 / math.sqrt(batch * lax.axis_size("dp") * length)
+    tap_terms = 3 * (margin + 1) * own
+    tap_rows = -(-tap_terms // 16) * 8
+    sums = sums.reshape(2, modes, count, own, LANES).transpose(0, 2, 1, 3, 4)
+    sums = sums.reshape(2, count, modes * own, LANES)
+    tap_sums = tap_sums.reshape(-1, count, own, LANES).transpose(1, 0, 2, 3)
+    tap_sums = tap_sums.reshape(count, tap_terms, LANES)
+    tap_sums = jnp.pad(tap_sums, ((0, 0), (0, 2 * tap_rows - tap_terms), (0, 0)))
+    tap_sums = tap_sums.reshape(count, 2, tap_rows, LANES).transpose(1, 0, 2, 3)
+    packed = jnp.concatenate([sums, tap_sums], axis=2)
+    half = packed.shape[2]
+    blocked = [vmem_like((count, half, LANES))] * 3
+    whole = [(2, modes * own, LANES), (2, count, tap_rows, LANES)]
+    results = [jax.ShapeDtypeStruct(shape, F32) for shape in whole]
+    landing = [vmem_like(shape) for shape in whole]
+    cores = lax.axis_size("dp")
+    if cores == 2:
+        reduced, filter_grad = comm_call(
+            end_kernel, 1, "sum_gradients", results, blocked + landing + [each, each, few]
+        )(packed)
+    else:
+        reduced = comm_call(
+            reduce_kernel,
+            1,
+            "reduce_sums",
+            jax.ShapeDtypeStruct((half, LANES), F32),
+            blocked + [each, few],
+        )(packed)
+        groups = [[j for j in range(cores) if j % 2 == i] for i in range(2)]
+        reduced = lax.psum(reduced, "dp", axis_index_groups=groups)
+        reduced, filter_grad = comm_call(
+            share_kernel, 2, "share_sums", results, landing + [each, few]
+        )(reduced)
+    factor = 1.0 / math.sqrt(batch * cores * length)
     reduced = reduced * factor
-    filter_grad = lax.all_gather(reduced[2 * modes :], "seq", axis=1)
+    filter_grad = filter_grad.transpose(1, 0, 2, 3).reshape(count, 2 * tap_rows, LANES)
+    filter_grad = filter_grad[:, :tap_terms] * factor
+    filter_grad = filter_grad.reshape(count, 3, margin + 1, own * LANES).transpose(1, 2, 0, 3)
     filter_grad = filter_grad.reshape(3, margin + 1, width)
     first_sum, second_sum = (
-        reduced[: 2 * modes].reshape(2, modes, own * LANES).transpose(0, 2, 1)
+        reduced.reshape(2, modes, own * LANES).transpose(0, 2, 1)
     )
     residue_grad = root * first_sum
     rate_grad = (

time: 203 us -> 127 us (0.63)
  blocking collectives: 119 us -> 0 us
  Pallas kernels: 49.8 us -> 111 us
  starting transfers between devices: 9.71 us -> 0 us
  waiting for transfers between devices: 9.4 us -> 0 us
  local copies, waits for them, and re-layouts: 8.88 us -> 12.3 us
    all_gather x2 -> x0, blocking collectives: 83.7 us -> none  [the longest x1 45.2 us: body(): everyone = lax.all_gather(mine, 'seq')]
    pallas_call x2, Pallas kernels: 15.4 us -> 76.5 us  [the longest x1 51.7 us: body(): comm_call(functools.partial(front_kernel, tokens, margin, modes, blocks,...]
    all_to_all x2 -> x0, blocking collectives: 32.1 us -> none  [swap(): lax.all_to_all(blocks, 'seq', split_axis=0, concat_axis=0, tiled=True)]
    all_to_all x1 -> x0, waiting for transfers between devices: 9.39 us -> none  [swap(): lax.all_to_all(blocks, 'seq', split_axis=0, concat_axis=0, tiled=True)]
    ppermute x2 -> x0, starting transfers between devices: 6.14 us -> none  [passed_along(): return lax.ppermute(shard, axis, pairs)]
    all_to_all x1 -> x0, starting transfers between devices: 3.57 us -> none  [swap(): lax.all_to_all(blocks, 'seq', split_axis=0, concat_axis=0, tiled=True)]
    psum x1 -> x0, blocking collectives: 3.52 us -> none  [body(): reduced = lax.psum(jnp.sum(swap(packed), axis=0), 'dp')]
  transfers between devices with their start and end apart: 3 -> 0, of which waited for: 1 -> 0; matrix products, arithmetic and copies ran while one was open for 2% -> 0% of each run, Pallas kernels for 0% -> 0%
where the time goes in v3:
time: 127 us; the launch traced here: 126 us
  Pallas kernels  111 us (87%)
  local copies, waits for them, and re-layouts  12.3 us (10%)
  other arithmetic  2.46 us (2%)
    pallas_call x1, Pallas kernels, body(): comm_call(functools.partial(front_kernel, tokens, margin, modes, blocks,...  51.7 us
    pallas_call x1, Pallas kernels, body(): pl.pallas_call(functools.partial(main_kernel, tokens, margin, modes, mode...  34.4 us
    pallas_call x1, Pallas kernels, body(): comm_call(end_kernel, 1, 'sum_gradients', results, blocked + landing + [e...  24.8 us
    slice x3, local copies, waits for them, and re-layouts, body(): x[0, :margin]  2.75 us

profile of v3, /device:TPU:0, one launch (start us, length us, event | category | flops | bytes accessed | tf_op | source)
XLA Modules:
  0.0 126.4 jit_solution(14230488706357208532)
XLA Ops:
  0.6 0.0 copy-start.2
  0.6 0.0 copy-start.3
  0.7 0.8 stack.15
  1.4 0.0 copy-done.2
  1.4 0.0 copy-done.3
  1.5 0.6 pad_maximum_fusion.3.mine
  2.1 0.8 slice.30
  3.0 0.9 fusion.8
  3.9 1.0 fusion.6
  4.9 0.1 pad_maximum_fusion.1
  5.0 0.0 copy-start.1
  5.0 0.7 reshape.54.after
  5.7 0.1 pad_maximum_fusion.2
  5.8 0.7 reshape.53.before
  6.5 0.0 copy-done.1
  6.5 0.8 reshape.55.taps
  7.2 51.7 %block_states.1 = (f32[2,16,32,128]{3,2,1,0:T(8,128)}, bf16[3,2,32,128]{3,2,1,0:T(8,128)(2,1)}, bf16[4,2,32,128]{3,2,1,0:T(8,128)(2,1)}, f32[4,16,2,8,128]{4,3,2,1,0:T(8,128)}) custom-call(bf16[1,128,4096]{2,1,0:T(8,128)(2,1)} %q.3, bf16[1,128,4096]{2,1,0:T(8,128)(2,1)} %k.3, bf16[1,128,4096]{2,1,0:T(8,128)(2,1)} %v.3, bf16[1,128,4096]{2,1,0:T(8,128)(2,1)} %c.3, ...), custom_call_target="tpu_custom_call" | custom-call | tf_op jit(solution)/shard_map/block_states/pallas_call | solution.py:451
  58.9 1.9 %slice_bitcast_fusion = (f32[16,32,128]{2,1,0:T(8,128)}, f32[16,32,128]{2,1,0:T(8,128)}) fusion(f32[2,16,32,128]{3,2,1,0:T(8,128)} %get-tuple-element.19), kind=kLoop, calls=%fused_computation.2 | loop fusion | bytes 1048576 | tf_op jit(solution)/shard_map/unstack | solution.py:472
  60.8 34.4 %mixer.1 = (bf16[1,128,4096]{2,1,0:T(8,128)(2,1)}, bf16[1,128,4096]{2,1,0:T(8,128)(2,1)}, bf16[1,128,4096]{2,1,0:T(8,128)(2,1)}, f32[2,16,32,128]{3,2,1,0:T(8,128)}, f32[3,3,32,128]{3,2,1,0:T(8,128)}) custom-call(bf16[1,128,4096]{2,1,0:T(8,128)(2,1)} %q.3, bf16[1,128,4096]{2,1,0:T(8,128)(2,1)} %k.3, bf16[1,128,4096]{2,1,0:T(8,128)(2,1)} %v.3, ...), custom_call_target="tpu_custom_call" | custom-call | tf_op jit(solution)/shard_map/mixer/pallas_call | solution.py:486
  95.2 0.9 copy.20
  96.1 0.0 copy-start
  96.1 0.1 copy.28
  96.2 0.9 copy-done
  97.1 0.3 copy.19
  97.4 0.9 pad_maximum_fusion.packed
  98.4 24.8 %sum_gradients.1 = (f32[2,32,128]{2,1,0:T(8,128)}, f32[2,16,16,128]{3,2,1,0:T(8,128)}) custom-call(f32[2,16,48,128]{3,2,1,0:T(8,128)} %pad_maximum_fusion.packed), custom_call_target="tpu_custom_call" | custom-call | tf_op jit(solution)/shard_map/sum_gradients/pallas_call | solution.py:520
  123.2 1.0 copy.23
  124.2 0.1 reshape.62
  124.3 0.0 copy-start.4
  124.3 0.7 copy-done.4
  125.0 0.6 fusion.2
  125.7 0.8 reshape.63
  (7 shorter events, 0.1 us)
Async XLA Ops:
  0.6 0.8 copy-start.2
  0.6 0.8 copy-start.3
  5.0 1.4 %copy-start.1 = (f32[3,3,4096]{2,1,0:T(4,128)S(1)}, f32[3,3,4096]{2,1,0:T(4,128)}, u32[]{:S(2)}) copy-start(f32[3,3,4096]{2,1,0:T(4,128)} %param.11) | copy-start | bytes 442372
  96.1 1.0 copy-start
  124.3 0.8 copy-start.4

commit v4 on v3

--- a/solution.py
+++ b/solution.py
@@ -37,24 +37,15 @@
     lax.fori_loop(0, tokens // 16, step, 0)
 
 
-def gather_rows(source, target, tokens):
+def gather_rows(source, target, tokens, base):
     def step(i, carry):
         start = pl.multiple_of(i * 16, 16)
         for s in range(GROUPS):
             piece = source[pl.ds(start * GROUPS + s, 16, stride=GROUPS), :]
-            target[0, pl.ds(start, 16), s * LANES : (s + 1) * LANES] = piece.astype(BF16)
+            target[0, pl.ds(start, 16), pl.ds(base + s * LANES, LANES)] = piece.astype(BF16)
         return carry
 
     lax.fori_loop(0, tokens // 16, step, 0)
-
-
-def load_inputs(tokens, margin, rows, before, after, wide):
-    for i in range(4):
-        spread_rows(rows[i], wide[i], margin, tokens)
-        for j in range(margin):
-            if i < 3:
-                wide[i][row(j), :] = before[i, j].astype(F32)
-            wide[i][row(margin + tokens + j), :] = after[i, j].astype(F32)
 
 
 def short_products(tokens, margin, taps, wide, gated, grad_mixed, keep):
@@ -77,19 +68,16 @@
     lax.fori_loop(0, tokens + margin, step, 0, unroll=2)
 
 
-def main_kernel(
-    tokens, margin, modes, part, q, k, v, c, before, after, taps, rate, weight, state,
+def main_block(
+    tokens, margin, modes, part, cols, base, taps, rate, weight, carry_of,
     dq, dk, dv, sums, tap_sums,
-    w0, w1, w2, w3, gated, grad_mixed, keys, values, mixed, grad_gated, trail, o0, o1, o2,
+    wide, gated, grad_mixed, keys, values, mixed, grad_gated, trail, outs,
 ):
-    wide = (w0, w1, w2, w3)
-    load_inputs(tokens, margin, (q, k, v, c), before, after, wide)
-    short_products(tokens, margin, taps, wide, gated, grad_mixed, (keys, values))
     zero = jnp.zeros((GROUPS, LANES), F32)
     for first in range(0, modes, part):
         some = range(first, first + part)
-        decay = [jnp.exp(-rate[n]) for n in some]
-        amount = [weight[n] for n in some]
+        decay = [jnp.exp(-rate[n, cols, :]) for n in some]
+        amount = [weight[n, cols, :] for n in some]
 
         def total_of(terms):
             terms = list(terms)
@@ -110,10 +98,10 @@
             mixed[row(t), :] = y
             return (x, tuple(dots[n] + g * x[n] for n in range(part)))
 
-        start = tuple(state[0, n, 0] for n in some)
+        start = tuple(carry_of(n, 0) for n in some)
         x, dots = lax.fori_loop(0, tokens, forward, (start, (zero,) * part), unroll=2)
         for n in range(part):
-            sums[0, first + n] = dots[n]
+            sums[0, first + n, cols, :] = dots[n]
         for t in range(tokens, tokens + margin):
             u = gated[row(t), :]
             x = tuple(decay[n] * x[n] + u for n in range(part))
@@ -134,11 +122,11 @@
             grad_gated[row(t), :] = y
             return (h, dots)
 
-        start = tuple(state[0, n, 1] for n in some)
+        start = tuple(carry_of(n, 1) for n in some)
         h, dots = lax.fori_loop(0, tokens, backward, (start, (zero,) * part), unroll=2)
         for n in range(part):
-            sums[1, first + n] = decay[n] * dots[n]
-        grow = [jnp.exp(rate[n]) for n in some]
+            sums[1, first + n, cols, :] = decay[n] * dots[n]
+        grow = [jnp.exp(rate[n, cols, :]) for n in some]
         h = start
         for t in range(tokens, tokens + margin):
             y = total_of(amount[n] * h[n] for n in range(part))
@@ -148,8 +136,7 @@
             g = grad_mixed[row(t), :]
             h = tuple((h[n] - g) * grow[n] for n in range(part))
 
-    filters = [[taps[i, j] for j in range(margin + 1)] for i in range(3)]
-    outs = (o0, o1, o2)
+    filters = [[taps[i, j, cols, :] for j in range(margin + 1)] for i in range(3)]
 
     def grads_at(t):
         m = rounded(mixed[row(t), :])
@@ -175,9 +162,9 @@
     later, dots = lax.fori_loop(0, tokens, finish, (later, (zero,) * (3 * (margin + 1))), unroll=2)
     for a in range(3):
         for j in range(margin + 1):
-            tap_sums[a, j] = dots[a * (margin + 1) + j]
+            tap_sums[a, j, cols, :] = dots[a * (margin + 1) + j]
     for source, target in zip(outs, (dq, dk, dv)):
-        gather_rows(source, target, tokens)
+        gather_rows(source, target, tokens, base)
 
 
 MESH = pl.DeviceIdType.MESH
@@ -249,38 +236,76 @@
     return remote(ref, ref, sems, d, {"dp": other_core()})
 
 
-def front_kernel(
-    tokens, margin, modes, blocks, own,
-    q, k, v, c, mine, before, after, taps,
-    modal, got_before, got_after, carried,
-    w0, w1, w2, w3, gated, grad_mixed, slots, table, left, right, state, got, sent, landed,
-    slot_sems, halo_sems, swap_sems, out_sems, back_sems,
+class Level:
+
+    def __init__(self, size, mine, device_of, source_of, target, sems):
+        self.size, self.mine, self.device_of = size, mine, device_of
+        self.source_of, self.target, self.sems = source_of, target, sems
+
+    def copies(self):
+        for d in range(1, self.size):
+            j = lax.rem(self.mine + d, self.size)
+            device = {"seq": self.device_of(j)}
+            yield remote(self.source_of(j), self.target.at[self.mine], self.sems, d, device)
+
+    def start(self):
+        for copy in self.copies():
+            copy.start()
+
+    def wait(self):
+        for copy in self.copies():
+            copy.wait()
+
+
+def mixer_kernel(
+    tokens, margin, modes, blocks, own, inner,
+    q, k, v, c, mine, taps,
+    dq, dk, dv, sums, tap_sums,
+    w0, w1, w2, w3, gated, grad_mixed, keys, values, mixed, grad_gated, trail, o0, o1, o2,
+    slots, table, before, after, left, right, state, got, total, planes, sent, landed,
+    slot_sems, halo_sems, swap_sems, out_sems, plane_sems, back_sems,
 ):
     me = lax.axis_index("seq")
     count = lax.axis_size("seq")
     core = core_of()
-    units = 2 * modes // count
+    outer = count // inner
+    per = modes // inner
+    low = lax.rem(me, inner)
+    high = lax.div(me, inner)
     wide = (w0, w1, w2, w3)
+    zero = jnp.zeros((GROUPS, LANES), F32)
     greet()
+    gathering = ToAll(lambda p: mine.at[core], slots.at[core], slot_sems)
+    gathering.start()
+    slots[core, me] = mine[core]
+    for b in range(blocks):
+        cols = slice(b * GROUPS, (b + 1) * GROUPS)
+        for i, x in enumerate((q, k, v, c)):
+            spread_rows(x, wide[i].at[b], margin, tokens, b * WIDE)
+            for j in range(margin):
+                if i < 3:
+                    before[i, j, cols, :] = wide[i][b, row(tokens + j), :]
+                after[i, j, cols, :] = wide[i][b, row(margin + j), :]
     halos = [
         remote(before, left, halo_sems, 0, {"seq": partner(1)}),
         remote(after, right, halo_sems, 1, {"seq": partner(count - 1)}),
     ]
     for copy in halos:
         copy.start()
-    gathering = ToAll(lambda p: mine.at[core], slots.at[core], slot_sems)
-    gathering.start()
-    slots[core, me] = mine[core]
-    for b in range(blocks):
-        for i, x in enumerate((q, k, v, c)):
-            spread_rows(x, wide[i].at[b], margin, tokens, b * WIDE)
     gathering.wait()
     copy = to_other_core(slots.at[core], swap_sems, 0)
     copy.start()
     for halo in halos:
         halo.wait()
-    got_before[...] = jnp.where(me > 0, left[...].astype(F32), 0.0).astype(BF16)
-    got_after[...] = jnp.where(me < count - 1, right[...].astype(F32), 0.0).astype(BF16)
+    for b in range(blocks):
+        cols = slice(b * GROUPS, (b + 1) * GROUPS)
+        for i in range(4):
+            for j in range(margin):
+                if i < 3:
+                    wide[i][b, row(j), :] = jnp.where(me > 0, left[i, j, cols, :], 0.0)
+                wide[i][b, row(margin + tokens + j), :] = jnp.where(
+                    me < count - 1, right[i, j, cols, :], 0.0
+                )
     copy.wait()
 
     def arrange(n, carry):
@@ -290,47 +315,69 @@
         return carry
 
     lax.fori_loop(0, modes, arrange, 0)
-    modal[...] = table[...]
-    zero = jnp.zeros((GROUPS, LANES), F32)
-
-    def out_copies(b):
-        return ToAll(lambda p: state.at[b, p], got.at[b], out_sems.at[b])
-
-    def back_copies(b):
-        return ToAll(lambda p: sent.at[b, p], landed.at[b], back_sems.at[b])
-
-    def combine(b):
-        out_copies(b).wait()
+    rate, weight = table.at[0], table.at[1]
+
+    def near(source, target, sems, b):
+        return Level(
+            inner, low, lambda j: high * inner + j, lambda j: source.at[b, j], target.at[b], sems.at[b]
+        )
+
+    def far(b):
+        def source_of(j):
+            return total.at[b, jnp.where(j > high, 0, 1)]
+
+        return Level(
+            outer, high, lambda j: j * inner + low, source_of, planes.at[b], plane_sems.at[b]
+        )
+
+    def power(n, cols, times):
+        return jnp.exp(-times * tokens * table[0, low * per + n, cols, :])
+
+    def add_group(b):
+        near(state, got, out_sems, b).wait()
         cols = slice(b * GROUPS, (b + 1) * GROUPS)
-        for unit in range(units):
-            which = me * units + unit
-            backward = lax.rem(which, 2)
-            factor = jnp.exp(-tokens * table[0, lax.div(which, 2), cols, :])
-
-            def step(p, total):
-                place = p + backward * (count - 1 - 2 * p)
-                sent[b, place, unit] = total
-                return factor * total + got[b, place, unit]
-
-            lax.fori_loop(0, count, step, zero, unroll=4)
-        back_copies(b).start()
-        landed[b, me] = sent[b, me]
+        for n in range(per):
+            factor = power(n, cols, 1)
+            ahead = got[b, 0, 0, n]
+            back = got[b, inner - 1, 1, n]
+            for j in range(1, inner):
+                ahead = factor * ahead + got[b, j, 0, n]
+                back = factor * back + got[b, inner - 1 - j, 1, n]
+            total[b, 0, n] = ahead
+            total[b, 1, n] = back
+        far(b).start()
+
+    def give_back(b):
+        far(b).wait()
+        cols = slice(b * GROUPS, (b + 1) * GROUPS)
+        for n in range(per):
+            factor = power(n, cols, 1)
+            jump = power(n, cols, inner)
+            ahead = lax.fori_loop(0, high, lambda z, x: jump * x + planes[b, z, n], zero)
+            back = lax.fori_loop(
+                high + 1, outer, lambda z, x: jump * x + planes[b, outer + high - z, n], zero
+            )
+            for j in range(inner):
+                sent[b, j, 0, n] = ahead
+                ahead = factor * ahead + got[b, j, 0, n]
+                sent[b, inner - 1 - j, 1, n] = back
+                back = factor * back + got[b, inner - 1 - j, 1, n]
+        near(sent, landed, back_sems, b).start()
+        landed[b, low] = sent[b, low]
 
     for b in range(blocks):
         cols = slice(b * GROUPS, (b + 1) * GROUPS)
-        mine_wide = [x.at[b] for x in wide]
-        for i in range(4):
-            for j in range(margin):
-                if i < 3:
-                    mine_wide[i][row(j), :] = got_before[i, j, cols, :].astype(F32)
-                mine_wide[i][row(margin + tokens + j), :] = got_after[i, j, cols, :].astype(F32)
-        short_products(tokens, margin, taps[:, :, cols, :], mine_wide, gated, grad_mixed, None)
-        decay = [jnp.exp(-table[0, n, cols, :]) for n in range(modes)]
+        u_ref, g_ref = gated.at[b], grad_mixed.at[b]
+        short_products(
+            tokens, margin, taps[:, :, cols, :], [x.at[b] for x in wide], u_ref, g_ref,
+            (keys.at[b], values.at[b]),
+        )
+        decay = [jnp.exp(-rate[n, cols, :]) for n in range(modes)]
 
         def step(t, carry):
             ahead, back = carry
-            u = gated[row(t), :]
-            g = grad_mixed[row(tokens - 1 - t), :]
+            u = u_ref[row(t), :]
+            g = g_ref[row(tokens - 1 - t), :]
             return (
                 tuple(decay[n] * ahead[n] + u for n in range(modes)),
                 tuple(decay[n] * back[n] + g for n in range(modes)),
@@ -339,16 +386,29 @@
         ends = lax.fori_loop(0, tokens, step, ((zero,) * modes, (zero,) * modes), unroll=2)
         for n in range(modes):
             for i in range(2):
-                unit = 2 * n + i
-                state[b, unit // units, unit % units] = ends[i][n]
-        out_copies(b).start()
-        got[b, me] = state[b, me]
+                state[b, n // per, i, n % per] = ends[i][n]
+        near(state, got, out_sems, b).start()
+        got[b, low] = state[b, low]
         if b > 0:
-            combine(b - 1)
-    combine(blocks - 1)
+            add_group(b - 1)
+        if b > 1:
+            give_back(b - 2)
+    add_group(blocks - 1)
+    if blocks > 1:
+        give_back(blocks - 2)
     for b in range(blocks):
-        back_copies(b).wait()
-    carried[...] = landed[...]
+        if blocks == 1:
+            give_back(b)
+        near(sent, landed, back_sems, b).wait()
+        main_block(
+            tokens, margin, modes, modes // 2, slice(b * GROUPS, (b + 1) * GROUPS), b * WIDE,
+            taps, rate, weight, lambda n, i: landed[b, n // per, i, n % per],
+            dq, dk, dv, sums, tap_sums,
+            [x.at[b] for x in wide], gated.at[b], grad_mixed.at[b], keys.at[b], values.at[b],
+            mixed, grad_gated, trail, (o0, o1, o2),
+        )
+        if b == 0 and blocks > 1:
+            give_back(blocks - 1)
 
 
 def reduce_part(packed, other, summed, got, sems, swap_sems):
@@ -425,20 +485,16 @@
     own = residue.shape[0] // LANES
     tiles = width // LANES
     blocks = width // WIDE
-    assert 2 * modes % count == 0
-    units = 2 * modes // count
+    inner = 4
+    assert count % inner == 0 and modes % inner == 0
+    outer, per = count // inner, modes // inner
     length = tokens * count
-    vmem = 56 << 20
 
     root = jnp.sqrt(-jnp.expm1(-2.0 * decay_rate))
     each = pltpu.SemaphoreType.DMA((2, count))
-    each_block = pltpu.SemaphoreType.DMA((blocks, 2, count))
     few = pltpu.SemaphoreType.DMA((2, 3))
     mine = jnp.stack([decay_rate.T, (residue * root).T]).reshape(2, modes, own, LANES)
     rows = (query_rows, key_rows, value_rows, cotangent)
-    before = jnp.stack([x[0, tokens - margin :] for x in rows[:3]])
-    before = before.reshape(3, margin, tiles, LANES)
-    after = jnp.stack([x[0, :margin] for x in rows]).reshape(4, margin, tiles, LANES)
     taps = short_filter.reshape(3, margin + 1, tiles, LANES)
 
     def scratch(n, *lead):
@@ -447,59 +503,34 @@
     def vmem_like(shape):
         return pltpu.VMEM(shape, F32)
 
-    moving = (blocks, count, units, GROUPS, LANES)
-    modal, before, after, state = comm_call(
-        functools.partial(front_kernel, tokens, margin, modes, blocks, own),
+    group = (blocks, inner, 2, per, GROUPS, LANES)
+    levels = pltpu.SemaphoreType.DMA((blocks, 2, inner))
+    far_level = pltpu.SemaphoreType.DMA((blocks, 2, outer))
+    halo = [vmem_like((i, margin, tiles, LANES)) for i in (3, 4)]
+    dq, dk, dv, sums, tap_sums = comm_call(
+        functools.partial(mixer_kernel, tokens, margin, modes, blocks, own, inner),
         0,
-        "block_states",
-        [
-            jax.ShapeDtypeStruct((2, modes, tiles, LANES), F32),
-            jax.ShapeDtypeStruct(before.shape, BF16),
-            jax.ShapeDtypeStruct(after.shape, BF16),
-            jax.ShapeDtypeStruct(moving, F32),
-        ],
-        [scratch(tokens + 2 * margin, blocks)] * 4
-        + [scratch(tokens + margin)] * 2
-        + [
-            vmem_like((2, count, modes, own, LANES)),
-            vmem_like((2, modes, tiles, LANES)),
-            pltpu.VMEM(before.shape, BF16),
-            pltpu.VMEM(after.shape, BF16),
-        ]
-        + [vmem_like(moving)] * 4
-        + [each, few, few, each_block, each_block],
-    )(*rows, mine, before, after, taps)
-    rate, weight = modal
-    state = state.reshape(blocks, modes, 2, GROUPS, LANES)
-
-    rows_spec = pl.BlockSpec((1, tokens, WIDE), lambda i: (0, 0, i))
-
-    def tile_spec(*lead):
-        zeros = (0,) * len(lead)
-        return pl.BlockSpec(lead + (GROUPS, LANES), lambda i: zeros + (i, 0))
-
-    state_spec = pl.BlockSpec((1, modes, 2, GROUPS, LANES), lambda i: (i, 0, 0, 0, 0))
-    params = pltpu.CompilerParams(vmem_limit_bytes=vmem)
-    head = [rows_spec] * 4 + [tile_spec(3, margin), tile_spec(4, margin), tile_spec(3, margin + 1), tile_spec(modes)]
-    wide = [scratch(tokens + 2 * margin)] * 4
-    shapes = [jax.ShapeDtypeStruct(query_rows.shape, BF16)] * 3
-    dq, dk, dv, sums, tap_sums = pl.pallas_call(
-        functools.partial(main_kernel, tokens, margin, modes, modes // 2),
-        grid=(blocks,),
-        in_specs=head + [tile_spec(modes), state_spec],
-        out_specs=[rows_spec] * 3 + [tile_spec(2, modes), tile_spec(3, margin + 1)],
-        out_shape=shapes
+        "mixer",
+        [jax.ShapeDtypeStruct(query_rows.shape, BF16)] * 3
         + [
             jax.ShapeDtypeStruct((2, modes, tiles, LANES), F32),
             jax.ShapeDtypeStruct((3, margin + 1, tiles, LANES), F32),
         ],
-        scratch_shapes=wide
-        + [scratch(tokens + margin)] * 6
+        [scratch(tokens + 2 * margin, blocks)] * 4
+        + [scratch(tokens + margin, blocks)] * 4
+        + [scratch(tokens + margin)] * 2
         + [scratch(tokens * modes // 2)]
-        + [scratch(tokens)] * 3,
-        compiler_params=params,
-        name="mixer",
-    )(*rows, before, after, taps, rate, weight, state)
+        + [scratch(tokens)] * 3
+        + [vmem_like((2, count, modes, own, LANES)), vmem_like((2, modes, tiles, LANES))]
+        + halo * 2
+        + [vmem_like(group)] * 2
+        + [
+            vmem_like((blocks, 2, per, GROUPS, LANES)),
+            vmem_like((blocks, outer, per, GROUPS, LANES)),
+        ]
+        + [vmem_like(group)] * 2
+        + [each, few, few, levels, far_level, levels],
+    )(*rows, mine, taps)
 
     tap_terms = 3 * (margin + 1) * own
     tap_rows = -(-tap_terms // 16) * 8

time: 127 us -> 107 us (0.84)
  Pallas kernels: 111 us -> 93 us
  local copies, waits for them, and re-layouts: 12.3 us -> 9.98 us
    pallas_call x2 -> x1, Pallas kernels: 86 us -> 67.8 us  [body(): comm_call(functools.partial(mixer_kernel, tokens, margin, modes, blocks,...]
    unnamed x10 -> x15, local copies, waits for them, and re-layouts: 1.65 us -> 5.1 us
    slice x3 -> x0, local copies, waits for them, and re-layouts: 2.75 us -> none  [body(): x[0, :margin]]
    another operation x1 -> x0, local copies, waits for them, and re-layouts: 1.88 us -> none  [body(): rate, weight = modal]
    reshape x2 -> x0, local copies, waits for them, and re-layouts: 1.35 us -> none  [the longest x1 0.69 us: body(): jnp.stack([x[0, :margin] for x in rows]).reshape(4, margin, tiles, LANES)]
where the time goes in v4:
time: 107 us
  Pallas kernels  93 us (87%)
  local copies, waits for them, and re-layouts  9.98 us (9%)
  other arithmetic  3.01 us (3%)
    pallas_call x1, Pallas kernels, body(): comm_call(functools.partial(mixer_kernel, tokens, margin, modes, blocks,...  67.8 us
    pallas_call x1, Pallas kernels, body(): comm_call(end_kernel, 1, 'sum_gradients', results, blocked + landing + [e...  25.2 us
    unnamed x15, local copies, waits for them, and re-layouts  5.1 us

profile of v4, /device:TPU:0, one launch (start us, length us, event | category | flops | bytes accessed | tf_op | source)
XLA Modules:
  0.0 106.8 jit_solution(600801382575304200)
XLA Ops:
  0.6 0.0 copy-start.5
  0.6 0.0 copy-start.4
  0.7 1.7 %reshape.47.taps = f32[3,3,32,128]{3,2,1,0:T(8,128)} reshape(f32[3,3,4096]{2,1,0:T(4,128)} %param.11) | data formatting | bytes 294912 | tf_op jit(solution)/shard_map/reshape | solution.py:498
  2.4 0.0 copy-done.5
  2.4 0.0 copy-done.4
  2.4 0.6 pad_maximum_fusion.1.mine
  3.1 67.8 %mixer.1 = (bf16[1,128,4096]{2,1,0:T(8,128)(2,1)}, bf16[1,128,4096]{2,1,0:T(8,128)(2,1)}, bf16[1,128,4096]{2,1,0:T(8,128)(2,1)}, f32[2,16,32,128]{3,2,1,0:T(8,128)}, f32[3,3,32,128]{3,2,1,0:T(8,128)}) custom-call(bf16[1,128,4096]{2,1,0:T(8,128)(2,1)} %q.1, bf16[1,128,4096]{2,1,0:T(8,128)(2,1)} %k.1, bf16[1,128,4096]{2,1,0:T(8,128)(2,1)} %v.1, ...), custom_call_target="tpu_custom_call" | custom-call | tf_op jit(solution)/shard_map/mixer/pallas_call | solution.py:510
  70.9 0.9 copy.20
  71.8 0.0 copy-start.3
  71.8 0.1 copy.28
  71.9 0.9 copy-done.3
  72.8 0.3 copy.19
  73.1 0.9 pad_maximum_fusion.packed
  74.0 25.2 %sum_gradients.1 = (f32[2,32,128]{2,1,0:T(8,128)}, f32[2,16,16,128]{3,2,1,0:T(8,128)}) custom-call(f32[2,16,48,128]{3,2,1,0:T(8,128)} %pad_maximum_fusion.packed), custom_call_target="tpu_custom_call" | custom-call | tf_op jit(solution)/shard_map/sum_gradients/pallas_call | solution.py:551
  99.3 0.8 broadcast_multiply_fusion
  100.1 0.0 copy-start.2
  100.1 0.6 fusion.2
  100.7 1.0 copy.23
  101.7 0.1 reshape.54
  101.8 0.8 reshape.55
  102.6 0.0 copy-done.2
  102.6 0.0 copy-start.1
  102.6 1.0 copy.32
  103.6 0.6 copy-done.1
  104.2 0.0 copy-start
  104.2 1.0 copy.33
  105.2 0.6 copy-done
  105.8 1.0 copy.34
  (7 shorter events, 0.1 us)
Async XLA Ops:
  0.6 1.7 %copy-start.5 = (f32[256,16]{0,1:T(8,128)S(1)}, f32[256,16]{0,1:T(8,128)}, u32[]{:S(2)}) copy-start(f32[256,16]{0,1:T(8,128)} %param.12) | copy-start | bytes 49156
  0.6 1.7 %copy-start.4 = (f32[256,16]{0,1:T(8,128)S(1)}, f32[256,16]{0,1:T(8,128)}, u32[]{:S(2)}) copy-start(f32[256,16]{0,1:T(8,128)} %param.13) | copy-start | bytes 49156
  71.8 1.0 copy-start.3
  100.1 2.5 %copy-start.2 = (bf16[1,128,4096]{2,1,0:T(8,128)(2,1)S(1)}, bf16[1,128,4096]{2,1,0:T(8,128)(2,1)}, u32[]{:S(2)}) copy-start(bf16[1,128,4096]{2,1,0:T(8,128)(2,1)} %get-tuple-element.28) | copy-start | bytes 3145732
  102.6 1.6 %copy-start.1 = (bf16[1,128,4096]{2,1,0:T(8,128)(2,1)S(1)}, bf16[1,128,4096]{2,1,0:T(8,128)(2,1)}, u32[]{:S(2)}) copy-start(bf16[1,128,4096]{2,1,0:T(8,128)(2,1)} %get-tuple-element.29) | copy-start | bytes 3145732
  104.2 1.6 %copy-start = (bf16[1,128,4096]{2,1,0:T(8,128)(2,1)S(1)}, bf16[1,128,4096]{2,1,0:T(8,128)(2,1)}, u32[]{:S(2)}) copy-start(bf16[1,128,4096]{2,1,0:T(8,128)(2,1)} %get-tuple-element.30) | copy-start | bytes 3145732

commit v5 on v4

--- a/solution.py
+++ b/solution.py
@@ -65,12 +65,12 @@
             keep[1][row(t), :] = shorted[2]
         return carry
 
-    lax.fori_loop(0, tokens + margin, step, 0, unroll=2)
+    lax.fori_loop(0, tokens + margin, step, 0, unroll=4)
 
 
 def main_block(
     tokens, margin, modes, part, cols, base, taps, rate, weight, carry_of,
-    dq, dk, dv, sums, tap_sums,
+    dq, dk, dv, put_sum, put_tap,
     wide, gated, grad_mixed, keys, values, mixed, grad_gated, trail, outs,
 ):
     zero = jnp.zeros((GROUPS, LANES), F32)
@@ -99,9 +99,9 @@
             return (x, tuple(dots[n] + g * x[n] for n in range(part)))
 
         start = tuple(carry_of(n, 0) for n in some)
-        x, dots = lax.fori_loop(0, tokens, forward, (start, (zero,) * part), unroll=2)
+        x, dots = lax.fori_loop(0, tokens, forward, (start, (zero,) * part), unroll=4)
         for n in range(part):
-            sums[0, first + n, cols, :] = dots[n]
+            put_sum(0, first + n, dots[n])
         for t in range(tokens, tokens + margin):
             u = gated[row(t), :]
             x = tuple(decay[n] * x[n] + u for n in range(part))
@@ -123,9 +123,9 @@
             return (h, dots)
 
         start = tuple(carry_of(n, 1) for n in some)
-        h, dots = lax.fori_loop(0, tokens, backward, (start, (zero,) * part), unroll=2)
+        h, dots = lax.fori_loop(0, tokens, backward, (start, (zero,) * part), unroll=4)
         for n in range(part):
-            sums[1, first + n, cols, :] = decay[n] * dots[n]
+            put_sum(1, first + n, decay[n] * dots[n])
         grow = [jnp.exp(rate[n, cols, :]) for n in some]
         h = start
         for t in range(tokens, tokens + margin):
@@ -159,10 +159,10 @@
         return (window[:margin], tuple(new))
 
     later = tuple(grads_at(tokens + j) for j in range(margin))
-    later, dots = lax.fori_loop(0, tokens, finish, (later, (zero,) * (3 * (margin + 1))), unroll=2)
+    later, dots = lax.fori_loop(0, tokens, finish, (later, (zero,) * (3 * (margin + 1))), unroll=4)
     for a in range(3):
         for j in range(margin + 1):
-            tap_sums[a, j, cols, :] = dots[a * (margin + 1) + j]
+            put_tap(a * (margin + 1) + j, dots[a * (margin + 1) + j])
     for source, target in zip(outs, (dq, dk, dv)):
         gather_rows(source, target, tokens, base)
 
@@ -183,6 +183,10 @@
     return lax.axis_index("dp") + 1 - 2 * core_of()
 
 
+def same_core(d):
+    return lax.rem(lax.axis_index("dp") + 2 * d, lax.axis_size("dp"))
+
+
 def greet():
     count = lax.axis_size("seq")
     barrier = pltpu.get_barrier_semaphore()
@@ -193,7 +197,10 @@
 
     lax.fori_loop(1, count, step, 0)
     pl.semaphore_signal(barrier, inc=1, device_id={"dp": other_core()}, device_id_type=MESH)
-    pl.semaphore_wait(barrier, count)
+    chips = lax.axis_size("dp") // 2
+    for d in range(1, chips):
+        pl.semaphore_signal(barrier, inc=1, device_id={"dp": same_core(d)}, device_id_type=MESH)
+    pl.semaphore_wait(barrier, count + chips - 1)
 
 
 def remote(source, target, sems, d, device):
@@ -245,7 +252,7 @@
     def copies(self):
         for d in range(1, self.size):
             j = lax.rem(self.mine + d, self.size)
-            device = {"seq": self.device_of(j)}
+            device = self.device_of(j)
             yield remote(self.source_of(j), self.target.at[self.mine], self.sems, d, device)
 
     def start(self):
@@ -258,12 +265,14 @@
 
 
 def mixer_kernel(
-    tokens, margin, modes, blocks, own, inner,
+    tokens, margin, modes, blocks, own, inner, scale,
     q, k, v, c, mine, taps,
     dq, dk, dv, sums, tap_sums,
     w0, w1, w2, w3, gated, grad_mixed, keys, values, mixed, grad_gated, trail, o0, o1, o2,
     slots, table, before, after, left, right, state, got, total, planes, sent, landed,
+    packed, other, summed, near_got, near_sum, far_got, chip_got, both, shared,
     slot_sems, halo_sems, swap_sems, out_sems, plane_sems, back_sems,
+    add_sems, near_sems, far_sems, chip_sems, share_sems,
 ):
     me = lax.axis_index("seq")
     count = lax.axis_size("seq")
@@ -274,6 +283,11 @@
     high = lax.div(me, inner)
     wide = (w0, w1, w2, w3)
     zero = jnp.zeros((GROUPS, LANES), F32)
+    per_block = outer // blocks
+    chips = lax.axis_size("dp") // 2
+    sum_rows = modes * own
+    tap_count = 3 * (margin + 1)
+    first_taps = (tap_count + 1) // 2
     greet()
     gathering = ToAll(lambda p: mine.at[core], slots.at[core], slot_sems)
     gathering.start()
@@ -319,7 +333,7 @@
 
     def near(source, target, sems, b):
         return Level(
-            inner, low, lambda j: high * inner + j, lambda j: source.at[b, j], target.at[b], sems.at[b]
+            inner, low, lambda j: {"seq": high * inner + j}, lambda j: source.at[b, j], target.at[b], sems.at[b]
         )
 
     def far(b):
@@ -327,7 +341,7 @@
             return total.at[b, jnp.where(j > high, 0, 1)]
 
         return Level(
-            outer, high, lambda j: j * inner + low, source_of, planes.at[b], plane_sems.at[b]
+            outer, high, lambda j: {"seq": j * inner + low}, source_of, planes.at[b], plane_sems.at[b]
         )
 
     def power(n, cols, times):
@@ -365,6 +379,54 @@
         near(sent, landed, back_sems, b).start()
         landed[b, low] = sent[b, low]
 
+    packed[...] = jnp.zeros_like(packed)
+
+    def put_rows(b, part, start, tile):
+        for o in range(per_block * inner):
+            target = packed.at[part, b * per_block + o // inner, o % inner]
+            target[start : start + own, :] = tile[o * own : (o + 1) * own, :]
+
+    def add_cores(b):
+        some = pl.ds(b * per_block, per_block)
+        return remote(
+            packed.at[1 - core, some], other.at[some], add_sems, b, {"dp": other_core()}
+        )
+
+    def near_sums(z):
+        return Level(
+            inner, low, lambda j: {"seq": high * inner + j},
+            lambda j: summed.at[z, j], near_got.at[z], near_sems.at[z],
+        )
+
+    far_sums = Level(
+        outer, high, lambda j: {"seq": j * inner + low}, lambda j: near_sum.at[j], far_got, far_sems
+    )
+
+    def pass_near(b):
+        add_cores(b).wait()
+        for z in range(b * per_block, (b + 1) * per_block):
+            summed[z] = packed[core, z] + other[z]
+            near_sums(z).start()
+            near_got[z, low] = summed[z, low]
+
+    def pass_far(b):
+        for z in range(b * per_block, (b + 1) * per_block):
+            near_sums(z).wait()
+            terms = near_got[z, 0]
+            for j in range(1, inner):
+                terms = terms + near_got[z, j]
+            near_sum[z] = terms
+
+            @pl.when(high == z)
+            def _():
+                far_got[z] = terms
+
+            @pl.when(high != z)
+            def _():
+                d = lax.rem(z - high + outer, outer)
+                device = {"seq": z * inner + low}
+                remote(near_sum.at[z], far_got.at[high], far_sems, d, device).start()
+
     for b in range(blocks):
         cols = slice(b * GROUPS, (b + 1) * GROUPS)
         u_ref, g_ref = gated.at[b], grad_mixed.at[b]
@@ -383,7 +445,7 @@
                 tuple(decay[n] * back[n] + g for n in range(modes)),
             )
 
-        ends = lax.fori_loop(0, tokens, step, ((zero,) * modes, (zero,) * modes), unroll=2)
+        ends = lax.fori_loop(0, tokens, step, ((zero,) * modes, (zero,) * modes), unroll=4)
         for n in range(modes):
             for i in range(2):
                 state[b, n // per, i, n % per] = ends[i][n]
@@ -400,68 +462,67 @@
         if blocks == 1:
             give_back(b)
         near(sent, landed, back_sems, b).wait()
+
+        def put_sum(i, n, tile):
+            put_rows(b, i, n * own, tile)
+
+        def put_tap(n, tile):
+            part, place = (0, n) if n < first_taps else (1, n - first_taps)
+            put_rows(b, part, sum_rows + place * own, tile)
+
         main_block(
             tokens, margin, modes, modes // 2, slice(b * GROUPS, (b + 1) * GROUPS), b * WIDE,
             taps, rate, weight, lambda n, i: landed[b, n // per, i, n % per],
-            dq, dk, dv, sums, tap_sums,
+            dq, dk, dv, put_sum, put_tap,
             [x.at[b] for x in wide], gated.at[b], grad_mixed.at[b], keys.at[b], values.at[b],
             mixed, grad_gated, trail, (o0, o1, o2),
         )
         if b == 0 and blocks > 1:
             give_back(blocks - 1)
-
-
-def reduce_part(packed, other, summed, got, sems, swap_sems):
-    me = lax.axis_index("seq")
-    core = core_of()
-    copy = remote(packed.at[1 - core], other, swap_sems, 0, {"dp": other_core()})
-    copy.start()
-    copy.wait()
-    summed[...] = packed[core] + other[...]
-    copies = ToAll(lambda p: summed.at[p], got, sems)
-    copies.start()
-    got[me] = summed[me]
-    copies.wait()
-    total = got[0]
-    for p in range(1, got.shape[0]):
-        total = total + got[p]
-    return total
-
-
-def share_part(total, sums, taps, both, slots, sems, swap_sems):
-    me = lax.axis_index("seq")
-    core = core_of()
-    count, tap_rows = slots.shape[1:3]
-    sum_rows = total.shape[0] - tap_rows
-    both[core] = total[:sum_rows]
-    slots[core, me] = total[sum_rows:]
-    copies = ToAll(lambda p: slots.at[core, me], slots.at[core], sems)
-    copies.start()
-    first = to_other_core(both.at[core], swap_sems, 1)
-    first.start()
-    copies.wait()
-    second = to_other_core(slots.at[core], swap_sems, 2)
-    second.start()
-    first.wait()
-    second.wait()
+        add_cores(b).start()
+        if b > 0:
+            pass_near(b - 1)
+        if b > 1:
+            pass_far(b - 2)
+    pass_near(blocks - 1)
+    if blocks > 1:
+        pass_far(blocks - 2)
+    pass_far(blocks - 1)
+    far_sums.wait()
+    total_rows = far_got[0]
+    for z in range(1, outer):
+        total_rows = total_rows + far_got[z]
+    if chips > 1:
+        chip = lax.div(lax.axis_index("dp"), 2)
+        chip_got[chip] = total_rows
+        level = Level(
+            chips, chip, lambda j: {"dp": 2 * j + core},
+            lambda j: chip_got.at[chip], chip_got, chip_sems,
+        )
+        level.start()
+        level.wait()
+        total_rows = chip_got[0]
+        for z in range(1, chips):
+            total_rows = total_rows + chip_got[z]
+    total_rows = total_rows * scale
+    shared[core, me] = total_rows[sum_rows:]
+    sharing = ToAll(lambda p: shared.at[core, me], shared.at[core], share_sems)
+    sharing.start()
+    both[core] = total_rows[:sum_rows]
+    swap_sums = to_other_core(both.at[core], swap_sems, 1)
+    swap_sums.start()
+    sharing.wait()
+    swap_taps = to_other_core(shared.at[core], swap_sems, 2)
+    swap_taps.start()
+    swap_sums.wait()
     sums[...] = both[...]
-    taps[...] = slots[...]
-
-
-def reduce_kernel(packed, out, other, summed, got, sems, swap_sems):
-    greet()
-    out[...] = reduce_part(packed, other, summed, got, sems, swap_sems)
-
-
-def share_kernel(half, sums, taps, both, slots, sems, swap_sems):
-    greet()
-    share_part(half[...], sums, taps, both, slots, sems, swap_sems)
-
-
-def end_kernel(packed, sums, taps, other, summed, got, both, slots, sems, share_sems, swap_sems):
-    greet()
-    total = reduce_part(packed, other, summed, got, sems, swap_sems)
-    share_part(total, sums, taps, both, slots, share_sems, swap_sems)
+    swap_taps.wait()
+    for n in range(tap_count):
+        part, place = (0, n) if n < first_taps else (1, n - first_taps)
+        for p in range(count):
+            tap_sums[n, p * own : (p + 1) * own, :] = shared[
+                part, p, place * own : (place + 1) * own, :
+            ]
 
 
 def comm_call(kernel, ident, name, shapes, scratch):
@@ -493,6 +554,11 @@
     root = jnp.sqrt(-jnp.expm1(-2.0 * decay_rate))
     each = pltpu.SemaphoreType.DMA((2, count))
     few = pltpu.SemaphoreType.DMA((2, 3))
+    cores = lax.axis_size("dp")
+    scale = 1.0 / math.sqrt(batch * cores * length)
+    tap_count = 3 * (margin + 1)
+    tap_rows = -(-((tap_count + 1) // 2 * own) // 8) * 8
+    rows_each = modes * own + tap_rows
     mine = jnp.stack([decay_rate.T, (residue * root).T]).reshape(2, modes, own, LANES)
     rows = (query_rows, key_rows, value_rows, cotangent)
     taps = short_filter.reshape(3, margin + 1, tiles, LANES)
@@ -508,13 +574,13 @@
     far_level = pltpu.SemaphoreType.DMA((blocks, 2, outer))
     halo = [vmem_like((i, margin, tiles, LANES)) for i in (3, 4)]
     dq, dk, dv, sums, tap_sums = comm_call(
-        functools.partial(mixer_kernel, tokens, margin, modes, blocks, own, inner),
+        functools.partial(mixer_kernel, tokens, margin, modes, blocks, own, inner, scale),
         0,
         "mixer",
         [jax.ShapeDtypeStruct(query_rows.shape, BF16)] * 3
         + [
-            jax.ShapeDtypeStruct((2, modes, tiles, LANES), F32),
-            jax.ShapeDtypeStruct((3, margin + 1, tiles, LANES), F32),
+            jax.ShapeDtypeStruct((2, modes * own, LANES), F32),
+            jax.ShapeDtypeStruct((tap_count, tiles, LANES), F32),
         ],
         [scratch(tokens + 2 * margin, blocks)] * 4
         + [scratch(tokens + margin, blocks)] * 4
@@ -529,49 +595,30 @@
             vmem_like((blocks, outer, per, GROUPS, LANES)),
         ]
         + [vmem_like(group)] * 2
-        + [each, few, few, levels, far_level, levels],
+        + [
+            vmem_like((2, outer, inner, rows_each, LANES)),
+            vmem_like((outer, inner, rows_each, LANES)),
+            vmem_like((outer, inner, rows_each, LANES)),
+            vmem_like((outer, inner, rows_each, LANES)),
+            vmem_like((outer, rows_each, LANES)),
+            vmem_like((outer, rows_each, LANES)),
+            vmem_like((max(cores // 2, 1), rows_each, LANES)),
+            vmem_like((2, modes * own, LANES)),
+            vmem_like((2, count, tap_rows, LANES)),
+        ]
+        + [each, few, few, levels, far_level, levels]
+        + [
+            pltpu.SemaphoreType.DMA((2, blocks)),
+            pltpu.SemaphoreType.DMA((outer, 2, inner)),
+            pltpu.SemaphoreType.DMA((2, outer)),
+            pltpu.SemaphoreType.DMA((2, max(cores // 2, 1))),
+            each,
+        ],
     )(*rows, mine, taps)
 
-    tap_terms = 3 * (margin + 1) * own
-    tap_rows = -(-tap_terms // 16) * 8
-    sums = sums.reshape(2, modes, count, own, LANES).transpose(0, 2, 1, 3, 4)
-    sums = sums.reshape(2, count, modes * own, LANES)
-    tap_sums = tap_sums.reshape(-1, count, own, LANES).transpose(1, 0, 2, 3)
-    tap_sums = tap_sums.reshape(count, tap_terms, LANES)
-    tap_sums = jnp.pad(tap_sums, ((0, 0), (0, 2 * tap_rows - tap_terms), (0, 0)))
-    tap_sums = tap_sums.reshape(count, 2, tap_rows, LANES).transpose(1, 0, 2, 3)
-    packed = jnp.concatenate([sums, tap_sums], axis=2)
-    half = packed.shape[2]
-    blocked = [vmem_like((count, half, LANES))] * 3
-    whole = [(2, modes * own, LANES), (2, count, tap_rows, LANES)]
-    results = [jax.ShapeDtypeStruct(shape, F32) for shape in whole]
-    landing = [vmem_like(shape) for shape in whole]
-    cores = lax.axis_size("dp")
-    if cores == 2:
-        reduced, filter_grad = comm_call(
-            end_kernel, 1, "sum_gradients", results, blocked + landing + [each, each, few]
-        )(packed)
-    else:
-        reduced = comm_call(
-            reduce_kernel,
-            1,
-            "reduce_sums",
-            jax.ShapeDtypeStruct((half, LANES), F32),
-            blocked + [each, few],
-        )(packed)
-        groups = [[j for j in range(cores) if j % 2 == i] for i in range(2)]
-        reduced = lax.psum(reduced, "dp", axis_index_groups=groups)
-        reduced, filter_grad = comm_call(
-            share_kernel, 2, "share_sums", results, landing + [each, few]
-        )(reduced)
-    factor = 1.0 / math.sqrt(batch * cores * length)
-    reduced = reduced * factor
-    filter_grad = filter_grad.transpose(1, 0, 2, 3).reshape(count, 2 * tap_rows, LANES)
-    filter_grad = filter_grad[:, :tap_terms] * factor
-    filter_grad = filter_grad.reshape(count, 3, margin + 1, own * LANES).transpose(1, 2, 0, 3)
-    filter_grad = filter_grad.reshape(3, margin + 1, width)
+    filter_grad = tap_sums.reshape(3, margin + 1, width)
     first_sum, second_sum = (
-        reduced.reshape(2, modes, own * LANES).transpose(0, 2, 1)
+        sums.reshape(2, modes, own * LANES).transpose(0, 2, 1)
     )
     residue_grad = root * first_sum
     rate_grad = (

time: 107 us -> 88.6 us (0.83)
  Pallas kernels: 93 us -> 78.2 us
  local copies, waits for them, and re-layouts: 9.98 us -> 8.24 us
  other arithmetic: 3.01 us -> 1.3 us
    pallas_call x1 -> x0, Pallas kernels: 25.2 us -> none  [body(): comm_call(end_kernel, 1, 'sum_gradients', results, blocked + landing + [e...]
    pallas_call x1, Pallas kernels: 67.8 us -> 78.2 us  [body(): comm_call(functools.partial(mixer_kernel, tokens, margin, modes, blocks,...]
    unnamed x15 -> x13, local copies, waits for them, and re-layouts: 5.1 us -> 4.96 us
where the time goes in v5:
time: 88.6 us; the launch traced here: 88.4 us
  Pallas kernels  78.2 us (88%)
  local copies, waits for them, and re-layouts  8.24 us (9%)
  other arithmetic  1.3 us (1%)
    pallas_call x1, Pallas kernels, body(): comm_call(functools.partial(mixer_kernel, tokens, margin, modes, blocks,...  78.2 us
    unnamed x13, local copies, waits for them, and re-layouts  4.96 us

profile of v5, /device:TPU:0, one launch (start us, length us, event | category | flops | bytes accessed | tf_op | source)
XLA Modules:
  0.0 88.4 jit_solution(15303132092397431094)
XLA Ops:
  0.6 0.0 copy-start.4
  0.6 0.0 copy-start.2
  0.7 1.7 %reshape.26.taps = f32[3,3,32,128]{3,2,1,0:T(8,128)} reshape(f32[3,3,4096]{2,1,0:T(4,128)} %param.11) | data formatting | bytes 294912 | tf_op jit(solution)/shard_map/reshape | solution.py:564
  2.4 0.0 copy-done.4
  2.4 0.0 copy-done.2
  2.4 0.6 pad_maximum_fusion.mine
  3.1 78.2 %mixer.1 = (bf16[1,128,4096]{2,1,0:T(8,128)(2,1)}, bf16[1,128,4096]{2,1,0:T(8,128)(2,1)}, bf16[1,128,4096]{2,1,0:T(8,128)(2,1)}, f32[2,32,128]{2,1,0:T(8,128)}, f32[9,32,128]{2,1,0:T(8,128)}) custom-call(bf16[1,128,4096]{2,1,0:T(8,128)(2,1)} %q.1, bf16[1,128,4096]{2,1,0:T(8,128)(2,1)} %k.1, bf16[1,128,4096]{2,1,0:T(8,128)(2,1)} %v.1, ...), custom_call_target="tpu_custom_call" | custom-call | tf_op jit(solution)/shard_map/mixer/pallas_call | solution.py:576
  81.2 0.0 copy-start.3
  81.2 0.8 reshape.28
  82.0 0.6 fusion.2
  82.7 0.0 copy-done.3
  82.7 0.7 reshape.27
  83.4 0.0 copy-start.1
  83.4 2.4 %copy.16 = bf16[1,128,4096]{2,1,0:T(8,128)(2,1)} copy(bf16[1,128,4096]{2,1,0:T(8,128)(2,1)} %get-tuple-element.24) | data formatting | bytes 2097152
  85.8 0.0 copy-done.1
  85.8 0.0 copy-start
  85.8 1.0 %copy.17 = bf16[1,128,4096]{2,1,0:T(8,128)(2,1)} copy(bf16[1,128,4096]{2,1,0:T(8,128)(2,1)S(1)} %copy-done.1) | data formatting | bytes 2097152
  86.8 0.6 copy-done
  87.4 1.0 %copy.18 = bf16[1,128,4096]{2,1,0:T(8,128)(2,1)} copy(bf16[1,128,4096]{2,1,0:T(8,128)(2,1)S(1)} %copy-done) | data formatting | bytes 2097152
  (3 shorter events, 0.1 us)
Async XLA Ops:
  0.6 1.7 %copy-start.4 = (f32[256,16]{0,1:T(8,128)S(1)}, f32[256,16]{0,1:T(8,128)}, u32[]{:S(2)}) copy-start(f32[256,16]{0,1:T(8,128)} %param.12) | copy-start | bytes 49156
  0.6 1.7 %copy-start.2 = (f32[256,16]{0,1:T(8,128)S(1)}, f32[256,16]{0,1:T(8,128)}, u32[]{:S(2)}) copy-start(f32[256,16]{0,1:T(8,128)} %param.13) | copy-start | bytes 49156
  81.2 1.5 %copy-start.3 = (f32[9,32,128]{2,1,0:T(8,128)S(1)}, f32[9,32,128]{2,1,0:T(8,128)}, u32[]{:S(2)}) copy-start(f32[9,32,128]{2,1,0:T(8,128)} %get-tuple-element.14) | copy-start | bytes 442372
  83.4 2.4 %copy-start.1 = (bf16[1,128,4096]{2,1,0:T(8,128)(2,1)S(1)}, bf16[1,128,4096]{2,1,0:T(8,128)(2,1)}, u32[]{:S(2)}) copy-start(bf16[1,128,4096]{2,1,0:T(8,128)(2,1)} %get-tuple-element.25) | copy-start | bytes 3145732
  85.8 1.6 %copy-start = (bf16[1,128,4096]{2,1,0:T(8,128)(2,1)S(1)}, bf16[1,128,4096]{2,1,0:T(8,128)(2,1)}, u32[]{:S(2)}) copy-start(bf16[1,128,4096]{2,1,0:T(8,128)(2,1)} %get-tuple-element.26) | copy-start | bytes 3145732

commit v6 on v5

--- a/solution.py
+++ b/solution.py
@@ -289,9 +289,12 @@
     tap_count = 3 * (margin + 1)
     first_taps = (tap_count + 1) // 2
     greet()
-    gathering = ToAll(lambda p: mine.at[core], slots.at[core], slot_sems)
-    gathering.start()
-    slots[core, me] = mine[core]
+    gathers = [
+        ToAll(lambda p, i=i: mine.at[i, core], slots.at[i, core], slot_sems.at[i]) for i in range(2)
+    ]
+    gathers[0].start()
+    for i in range(2):
+        slots[i, core, me] = mine[i, core]
     for b in range(blocks):
         cols = slice(b * GROUPS, (b + 1) * GROUPS)
         for i, x in enumerate((q, k, v, c)):
@@ -306,9 +309,6 @@
     ]
     for copy in halos:
         copy.start()
-    gathering.wait()
-    copy = to_other_core(slots.at[core], swap_sems, 0)
-    copy.start()
     for halo in halos:
         halo.wait()
     for b in range(blocks):
@@ -320,15 +320,30 @@
                 wide[i][b, row(margin + tokens + j), :] = jnp.where(
                     me < count - 1, right[i, j, cols, :], 0.0
                 )
-    copy.wait()
-
-    def arrange(n, carry):
-        for i in range(2):
-            for p in range(count):
-                table[i, n, p * own : (p + 1) * own, :] = slots[i, p, n]
-        return carry
-
-    lax.fori_loop(0, modes, arrange, 0)
+    for b in range(blocks):
+        short_products(
+            tokens, margin, taps[:, :, b * GROUPS : (b + 1) * GROUPS, :],
+            [x.at[b] for x in wide], gated.at[b], grad_mixed.at[b], (keys.at[b], values.at[b]),
+        )
+
+    def arrange(i):
+        copy = to_other_core(slots.at[i, core], swap_sems, 3 * i)
+        copy.start()
+        copy.wait()
+        part = modes // 2
+
+        def step(n, carry):
+            for side in range(2):
+                for p in range(count):
+                    piece = slots[i, side, p, n]
+                    table[i, side * part + n, p * own : (p + 1) * own, :] = piece
+            return carry
+
+        lax.fori_loop(0, part, step, 0)
+
+    gathers[0].wait()
+    gathers[1].start()
+    arrange(0)
     rate, weight = table.at[0], table.at[1]
 
     def near(source, target, sems, b):
@@ -430,10 +445,6 @@
     for b in range(blocks):
         cols = slice(b * GROUPS, (b + 1) * GROUPS)
         u_ref, g_ref = gated.at[b], grad_mixed.at[b]
-        short_products(
-            tokens, margin, taps[:, :, cols, :], [x.at[b] for x in wide], u_ref, g_ref,
-            (keys.at[b], values.at[b]),
-        )
         decay = [jnp.exp(-rate[n, cols, :]) for n in range(modes)]
 
         def step(t, carry):
@@ -458,6 +469,8 @@
     add_group(blocks - 1)
     if blocks > 1:
         give_back(blocks - 2)
+    gathers[1].wait()
+    arrange(1)
     for b in range(blocks):
         if blocks == 1:
             give_back(b)
@@ -553,13 +566,14 @@
 
     root = jnp.sqrt(-jnp.expm1(-2.0 * decay_rate))
     each = pltpu.SemaphoreType.DMA((2, count))
-    few = pltpu.SemaphoreType.DMA((2, 3))
+    few = pltpu.SemaphoreType.DMA((2, 4))
+    each_twice = pltpu.SemaphoreType.DMA((2, 2, count))
     cores = lax.axis_size("dp")
     scale = 1.0 / math.sqrt(batch * cores * length)
     tap_count = 3 * (margin + 1)
     tap_rows = -(-((tap_count + 1) // 2 * own) // 8) * 8
     rows_each = modes * own + tap_rows
-    mine = jnp.stack([decay_rate.T, (residue * root).T]).reshape(2, modes, own, LANES)
+    mine = jnp.stack([decay_rate.T, (residue * root).T]).reshape(2, 2, modes // 2, own, LANES)
     rows = (query_rows, key_rows, value_rows, cotangent)
     taps = short_filter.reshape(3, margin + 1, tiles, LANES)
 
@@ -587,7 +601,7 @@
         + [scratch(tokens + margin)] * 2
         + [scratch(tokens * modes // 2)]
         + [scratch(tokens)] * 3
-        + [vmem_like((2, count, modes, own, LANES)), vmem_like((2, modes, tiles, LANES))]
+        + [vmem_like((2, 2, count, modes // 2, own, LANES)), vmem_like((2, modes, tiles, LANES))]
         + halo * 2
         + [vmem_like(group)] * 2
         + [
@@ -606,7 +620,7 @@
             vmem_like((2, modes * own, LANES)),
             vmem_like((2, count, tap_rows, LANES)),
         ]
-        + [each, few, few, levels, far_level, levels]
+        + [each_twice, few, few, levels, far_level, levels]
         + [
             pltpu.SemaphoreType.DMA((2, blocks)),
             pltpu.SemaphoreType.DMA((outer, 2, inner)),

time: 88.6 us -> 89.3 us (level)
  no operation moved by 1% of the time
where the time goes in v6:
time: 89.3 us; the launch traced here: 89.1 us
  Pallas kernels  78.8 us (88%)
  local copies, waits for them, and re-layouts  8.24 us (9%)
  other arithmetic  1.3 us (1%)
    pallas_call x1, Pallas kernels, body(): comm_call(functools.partial(mixer_kernel, tokens, margin, modes, blocks,...  78.8 us
    unnamed x13, local copies, waits for them, and re-layouts  4.96 us

profile of v6, /device:TPU:0, one launch (start us, length us, event | category | flops | bytes accessed | tf_op | source)
XLA Modules:
  0.0 89.1 jit_solution(11219403555358207161)
XLA Ops:
  0.6 0.0 copy-start.4
  0.6 0.0 copy-start.2
  0.7 1.7 %reshape.26.taps = f32[3,3,32,128]{3,2,1,0:T(8,128)} reshape(f32[3,3,4096]{2,1,0:T(4,128)} %param.11) | data formatting | bytes 294912 | tf_op jit(solution)/shard_map/reshape | solution.py:578
  2.4 0.0 copy-done.4
  2.4 0.0 copy-done.2
  2.4 0.6 pad_maximum_fusion.mine
  3.1 78.8 %mixer.1 = (bf16[1,128,4096]{2,1,0:T(8,128)(2,1)}, bf16[1,128,4096]{2,1,0:T(8,128)(2,1)}, bf16[1,128,4096]{2,1,0:T(8,128)(2,1)}, f32[2,32,128]{2,1,0:T(8,128)}, f32[9,32,128]{2,1,0:T(8,128)}) custom-call(bf16[1,128,4096]{2,1,0:T(8,128)(2,1)} %q.1, bf16[1,128,4096]{2,1,0:T(8,128)(2,1)} %k.1, bf16[1,128,4096]{2,1,0:T(8,128)(2,1)} %v.1, ...), custom_call_target="tpu_custom_call" | custom-call | tf_op jit(solution)/shard_map/mixer/pallas_call | solution.py:590
  81.9 0.0 copy-start.3
  81.9 0.8 reshape.28
  82.7 0.6 fusion.2
  83.4 0.0 copy-done.3
  83.4 0.7 reshape.27
  84.1 0.0 copy-start.1
  84.1 2.4 %copy.16 = bf16[1,128,4096]{2,1,0:T(8,128)(2,1)} copy(bf16[1,128,4096]{2,1,0:T(8,128)(2,1)} %get-tuple-element.24) | data formatting | bytes 2097152
  86.5 0.0 copy-done.1
  86.5 0.0 copy-start
  86.5 1.0 %copy.17 = bf16[1,128,4096]{2,1,0:T(8,128)(2,1)} copy(bf16[1,128,4096]{2,1,0:T(8,128)(2,1)S(1)} %copy-done.1) | data formatting | bytes 2097152
  87.5 0.6 copy-done
  88.1 1.0 %copy.18 = bf16[1,128,4096]{2,1,0:T(8,128)(2,1)} copy(bf16[1,128,4096]{2,1,0:T(8,128)(2,1)S(1)} %copy-done) | data formatting | bytes 2097152
  (3 shorter events, 0.1 us)
Async XLA Ops:
  0.6 1.7 %copy-start.4 = (f32[256,16]{0,1:T(8,128)S(1)}, f32[256,16]{0,1:T(8,128)}, u32[]{:S(2)}) copy-start(f32[256,16]{0,1:T(8,128)} %param.12) | copy-start | bytes 49156
  0.6 1.7 %copy-start.2 = (f32[256,16]{0,1:T(8,128)S(1)}, f32[256,16]{0,1:T(8,128)}, u32[]{:S(2)}) copy-start(f32[256,16]{0,1:T(8,128)} %param.13) | copy-start | bytes 49156
  81.9 1.5 %copy-start.3 = (f32[9,32,128]{2,1,0:T(8,128)S(1)}, f32[9,32,128]{2,1,0:T(8,128)}, u32[]{:S(2)}) copy-start(f32[9,32,128]{2,1,0:T(8,128)} %get-tuple-element.14) | copy-start | bytes 442372
  84.1 2.4 %copy-start.1 = (bf16[1,128,4096]{2,1,0:T(8,128)(2,1)S(1)}, bf16[1,128,4096]{2,1,0:T(8,128)(2,1)}, u32[]{:S(2)}) copy-start(bf16[1,128,4096]{2,1,0:T(8,128)(2,1)} %get-tuple-element.25) | copy-start | bytes 3145732
  86.5 1.6 %copy-start = (bf16[1,128,4096]{2,1,0:T(8,128)(2,1)S(1)}, bf16[1,128,4096]{2,1,0:T(8,128)(2,1)}, u32[]{:S(2)}) copy-start(bf16[1,128,4096]{2,1,0:T(8,128)(2,1)} %get-tuple-element.26) | copy-start | bytes 3145732
